TPU v7x, 256 devices: a whole 4x4x8 slice. The times are simulated.
256 devices in a mesh: trial: 2 (over y_hi), row: 8 (over y_lo, x), col: 16 (over z, core).
Axes of the slice: x: 4, y: 4 (y_hi: 2, y_lo: 2; y = y_hi * 2 + y_lo), z: 8, core: 2. Of those that a mesh axis runs over, the one named last changes fastest.
Arguments:
- layer_input_matrix: bfloat16 [8, 512, 5120], P('trial', 'row', 'col'), may hold values from -6 to 6
- output_gradient_matrix: bfloat16 [8, 512, 25600], P('trial', 'col', 'row'), may hold values from -6 to 6
- fixed_weight_matrix: bfloat16 [5120, 25600], P('col', 'row'), may hold values from -0.078125 to 0.078125
- adapter_left_matrices: bfloat16 [8, 5120, 1024], P('trial', 'col'), may hold values from -0.078125 to 0.078125
- adapter_right_matrices: bfloat16 [8, 1024, 25600], P('trial', 'col', 'row'), may hold values from -0.1875 to 0.1875
- chosen_adapter_entry: int32 [8], P('trial'), may hold values from 0 to 7, as said below
- valid_token_counts: int32 [8], P('trial'), may hold values from 128 to 512, as said below
Outputs:
- grad_input: bfloat16 [8, 512, 5120], P('trial', 'row', 'col')
- grad_a: float32 [8, 5120, 1024], P('trial', 'col', 'row')
- grad_b: float32 [8, 1024, 25600], P('trial', 'col', 'row')
Inputs may be any that keep to these rules, and one draw needn't show every extreme that they name: `chosen_adapter_entry`: for each index g of trial, the entries 4 g to 4 g + 3 are a permutation of those same numbers. `valid_token_counts`: every entry is a multiple of 128; some slot has all 512 tokens valid.
All inputs are finite; a program needn't handle non-finite values.
Results may differ from a plain program's by a relative error of at most 0.004.
Values may be sent and summed in bfloat16 or wider, within the bound.
No kernel may reach another device: no remote copies, remote signals or barrier semaphores. Data moves between devices by JAX's collectives and lax.ppermute only.
A program may use at most 128 MiB of HBM per device.

v0:
```python
import jax
import jax.numpy as jnp
from jax import lax
from jax.sharding import PartitionSpec as P


def contract_rows(left, right):
    return lax.dot_general(
        left, right, (((0,), (0,)), ((), ())), preferred_element_type=jnp.float32
    )


def contract_cols(left, right):
    return lax.dot_general(
        left, right, (((1,), (1,)), ((), ())), preferred_element_type=jnp.float32
    )


def body(
    layer_input_matrix,
    output_gradient_matrix,
    fixed_weight_matrix,
    adapter_left_matrices,
    adapter_right_matrices,
    chosen_adapter_entry,
    valid_token_counts,
):
    slots = layer_input_matrix.shape[0]
    dy_rows = output_gradient_matrix.shape[1]
    experiment_start_shift = lax.axis_index("trial") * slots
    col_start = lax.axis_index("col") * dy_rows
    grads_in = []
    grads_a = None
    grads_b = None
    for experiment_slot_place in range(slots):
        experiment_within_group = (
            chosen_adapter_entry[experiment_slot_place] - experiment_start_shift
        )
        factor_a = jnp.take(adapter_left_matrices, experiment_within_group, axis=0)
        up_factor = jnp.take(adapter_right_matrices, experiment_within_group, axis=0)
        length = valid_token_counts[experiment_slot_place]
        positions = col_start + jnp.arange(dy_rows, dtype=jnp.int32)
        upstream = jnp.where(
            (positions < length)[:, None],
            output_gradient_matrix[experiment_slot_place],
            jnp.zeros((), output_gradient_matrix.dtype),
        )
        acts = layer_input_matrix[experiment_slot_place]
        hidden_term = jnp.dot(acts, factor_a, preferred_element_type=jnp.float32)
        hidden = lax.psum_scatter(hidden_term, "col", scatter_dimension=1, tiled=True).astype(
            jnp.bfloat16
        )
        hidden_all = lax.all_gather(hidden, "row", axis=0, tiled=True)
        piece = lax.all_gather(upstream, "col", axis=0, tiled=True)
        grad_part = contract_rows(hidden_all, piece)
        main_terms = contract_cols(piece, fixed_weight_matrix)
        side_terms = contract_cols(piece, up_factor)
        input_part = lax.psum_scatter(main_terms, "row", scatter_dimension=0, tiled=True)
        factor_part = lax.psum_scatter(side_terms, "row", scatter_dimension=0, tiled=True)
        factor_grad = factor_part.astype(jnp.bfloat16)
        factor_full = lax.all_gather(factor_grad, "col", axis=1, tiled=True)
        grad_in = (input_part + contract_cols(factor_full, factor_a)).astype(jnp.bfloat16)
        grads_in.append(grad_in)
        scale = lax.rsqrt(length.astype(jnp.float32))
        grad_a_term = contract_rows(acts, factor_full)
        grad_a = lax.psum_scatter(grad_a_term, "row", scatter_dimension=1, tiled=True) * scale
        grad_b = grad_part * scale
        if grads_a is None:
            grads_a = jnp.zeros((slots,) + grad_a.shape, jnp.float32)
            grads_b = jnp.zeros((slots,) + grad_b.shape, jnp.float32)
        grads_a = grads_a.at[experiment_within_group].set(grad_a)
        grads_b = grads_b.at[experiment_within_group].set(grad_b)
    return (jnp.stack(grads_in), grads_a, grads_b)


def solution(mesh):
    return jax.shard_map(
        body,
        mesh=mesh,
        in_specs=(
            P("trial", "row", "col"),
            P("trial", "col", "row"),
            P("col", "row"),
            P("trial", "col", None),
            P("trial", "col", "row"),
            P("trial"),
            P("trial"),
        ),
        out_specs=(P("trial", "row", "col"), P("trial", "col", "row"), P("trial", "col", "row")),
        check_vma=False,
    )
```

profile of v0, /device:TPU:1, one launch (start us, length us, event | category | flops | bytes accessed | tf_op | source)
XLA Modules:
  0.0 927.5 jit_solution(15517150230009191680)
XLA Ops:
  18.8 39.9 %all-gather.5.cloned.1.call-done = bf16[512,3200]{1,0:T(8,128)(2,1)} async-done(((bf16[32,3200]{1,0:T(8,128)(2,1)}), bf16[512,3200]{1,0:T(8,128)(2,1)}) %all-gather.5.cloned.1.call-update) | async-done | bytes 3276816 | tf_op jit(solution)/shard_map/all_gather | solution.py:54
  62.5 38.5 %all-gather.7.cloned.1.call-done = bf16[512,3200]{1,0:T(8,128)(2,1)} async-done(((bf16[32,3200]{1,0:T(8,128)(2,1)}), bf16[512,3200]{1,0:T(8,128)(2,1)}) %all-gather.7.cloned.1.call-update) | async-done | bytes 3276816 | tf_op jit(solution)/shard_map/all_gather | solution.py:54
  101.0 3.7 fusion.32
  104.8 37.9 %all-gather.9.cloned.1.call-done = bf16[512,3200]{1,0:T(8,128)(2,1)} async-done(((bf16[32,3200]{1,0:T(8,128)(2,1)}), bf16[512,3200]{1,0:T(8,128)(2,1)}) %all-gather.9.cloned.1.call-update) | async-done | bytes 3276816 | tf_op jit(solution)/shard_map/all_gather | solution.py:54
  142.7 3.7 fusion.30
  157.0 27.3 %all-gather.11.cloned.1.call-done = bf16[512,3200]{1,0:T(8,128)(2,1)} async-done(((bf16[32,3200]{1,0:T(8,128)(2,1)}), bf16[512,3200]{1,0:T(8,128)(2,1)}) %all-gather.11.cloned.1.call-update) | async-done | bytes 3276816 | tf_op jit(solution)/shard_map/all_gather | solution.py:54
  184.3 3.7 fusion.28
  188.1 4.7 fusion.111
  192.9 4.7 fusion.110
  197.7 4.7 fusion.109
  202.5 4.7 fusion.112
  207.2 12.1 %reduce-scatter.27.cloned.1.call-done = f32[64,64]{1,0:T(8,128)} async-done(((f32[512,64]{1,0:T(8,128)}), f32[64,64]{1,0:T(8,128)}) %reduce-scatter.27.cloned.1.call-update) | async-done | bytes 16400 | tf_op jit(solution)/shard_map/reduce_scatter | solution.py:59
  220.1 24.1 %all_gather.37 = bf16[64,1024]{0,1:T(8,128)(2,1)S(1)} all-gather(bf16[64,64]{0,1:T(8,128)(2,1)S(1)} %copy.14), channel_id=1, replica_groups=mesh['trial'=2,'row'=8,'col'=16] {'col'}, dimensions={1}, use_global_device_ids=true | all-gather | bytes 139264 | tf_op jit(solution)/shard_map/all_gather | solution.py:61
  245.8 14.7 %reduce-scatter.31.cloned.1.call-done = f32[64,64]{1,0:T(8,128)} async-done(((f32[512,64]{1,0:T(8,128)}), f32[64,64]{1,0:T(8,128)}) %reduce-scatter.31.cloned.1.call-update) | async-done | bytes 16400 | tf_op jit(solution)/shard_map/reduce_scatter | solution.py:59
  261.3 24.1 %all_gather.39 = bf16[64,1024]{0,1:T(8,128)(2,1)S(1)} all-gather(bf16[64,64]{0,1:T(8,128)(2,1)S(1)} %copy.15), channel_id=1, replica_groups=mesh['trial'=2,'row'=8,'col'=16] {'col'}, dimensions={1}, use_global_device_ids=true | all-gather | bytes 139264 | tf_op jit(solution)/shard_map/all_gather | solution.py:61
  286.9 14.6 %reduce-scatter.35.cloned.1.call-done = f32[64,64]{1,0:T(8,128)} async-done(((f32[512,64]{1,0:T(8,128)}), f32[64,64]{1,0:T(8,128)}) %reduce-scatter.35.cloned.1.call-update) | async-done | bytes 16400 | tf_op jit(solution)/shard_map/reduce_scatter | solution.py:59
  302.4 24.1 %all_gather.41 = bf16[64,1024]{0,1:T(8,128)(2,1)S(1)} all-gather(bf16[64,64]{0,1:T(8,128)(2,1)S(1)} %copy.16), channel_id=1, replica_groups=mesh['trial'=2,'row'=8,'col'=16] {'col'}, dimensions={1}, use_global_device_ids=true | all-gather | bytes 139264 | tf_op jit(solution)/shard_map/all_gather | solution.py:61
  331.3 31.5 %reduce-scatter.49.cloned.1.call-done = f32[64,64]{1,0:T(8,128)} async-done(((f32[1024,64]{1,0:T(8,128)}), f32[64,64]{1,0:T(8,128)}) %reduce-scatter.49.cloned.1.call-update) | async-done | bytes 16400
  363.7 57.2 %reduce-scatter.51.cloned.1.call-done = f32[64,64]{1,0:T(8,128)} async-done(((f32[1024,64]{1,0:T(8,128)}), f32[64,64]{1,0:T(8,128)}) %reduce-scatter.51.cloned.1.call-update) | async-done | bytes 16400
  421.7 56.5 %reduce-scatter.53.cloned.1.call-done = f32[64,64]{1,0:T(8,128)} async-done(((f32[1024,64]{1,0:T(8,128)}), f32[64,64]{1,0:T(8,128)}) %reduce-scatter.53.cloned.1.call-update) | async-done | bytes 16400
  479.1 56.9 %reduce-scatter.55.cloned.1.call-done = f32[64,64]{1,0:T(8,128)} async-done(((f32[1024,64]{1,0:T(8,128)}), f32[64,64]{1,0:T(8,128)}) %reduce-scatter.55.cloned.1.call-update) | async-done | bytes 16400
  536.8 24.1 %all_gather.44 = bf16[512,64]{1,0:T(8,128)(2,1)} all-gather(bf16[64,64]{1,0:T(8,128)(2,1)S(1)} %copy.19), channel_id=1, replica_groups=mesh['trial'=2,'row'=8,'col'=16] {'row'}, dimensions={0}, use_global_device_ids=true | all-gather | bytes 73728 | tf_op jit(solution)/shard_map/all_gather | solution.py:53
  560.9 23.2 %all_gather.45 = bf16[512,64]{1,0:T(8,128)(2,1)S(1)} all-gather(bf16[64,64]{1,0:T(8,128)(2,1)S(1)} %copy.21), channel_id=1, replica_groups=mesh['trial'=2,'row'=8,'col'=16] {'row'}, dimensions={0}, use_global_device_ids=true | all-gather | bytes 73728 | tf_op jit(solution)/shard_map/all_gather | solution.py:53
  584.1 22.6 %all_gather.46 = bf16[512,64]{1,0:T(8,128)(2,1)S(1)} all-gather(bf16[64,64]{1,0:T(8,128)(2,1)S(1)} %copy.23), channel_id=1, replica_groups=mesh['trial'=2,'row'=8,'col'=16] {'row'}, dimensions={0}, use_global_device_ids=true | all-gather | bytes 73728 | tf_op jit(solution)/shard_map/all_gather | solution.py:53
  606.8 22.4 %all_gather.47 = bf16[512,64]{1,0:T(8,128)(2,1)S(1)} all-gather(bf16[64,64]{1,0:T(8,128)(2,1)S(1)} %copy.25), channel_id=1, replica_groups=mesh['trial'=2,'row'=8,'col'=16] {'row'}, dimensions={0}, use_global_device_ids=true | all-gather | bytes 73728 | tf_op jit(solution)/shard_map/all_gather | solution.py:53
  630.0 41.4 %all_gather.43 = bf16[64,1024]{0,1:T(8,128)(2,1)S(1)} all-gather(bf16[64,64]{0,1:T(8,128)(2,1)S(1)} %copy.17), channel_id=1, replica_groups=mesh['trial'=2,'row'=8,'col'=16] {'col'}, dimensions={1}, use_global_device_ids=true | all-gather | bytes 139264 | tf_op jit(solution)/shard_map/all_gather | solution.py:61
  693.5 7.9 reduce-scatter.25.cloned.1.call-done
  702.8 40.8 %reduce-scatter.37.cloned.1.call-done = f32[64,320]{1,0:T(8,128)} async-done(((f32[512,320]{1,0:T(8,128)}), f32[64,320]{1,0:T(8,128)}) %reduce-scatter.37.cloned.1.call-update) | async-done | bytes 81936 | tf_op jit(solution)/shard_map/reduce_scatter | solution.py:58
  745.8 41.6 %reduce-scatter.41.cloned.1.call-done = f32[320,128]{1,0:T(8,128)} async-done(((f32[320,1024]{1,0:T(8,128)}), f32[320,128]{1,0:T(8,128)}) %reduce-scatter.41.cloned.1.call-update) | async-done | bytes 163856 | tf_op jit(solution)/shard_map/reduce_scatter | solution.py:66
  789.1 41.9 %reduce-scatter.43.cloned.1.call-done = f32[320,128]{1,0:T(8,128)} async-done(((f32[320,1024]{1,0:T(8,128)}), f32[320,128]{1,0:T(8,128)}) %reduce-scatter.43.cloned.1.call-update) | async-done | bytes 163856 | tf_op jit(solution)/shard_map/reduce_scatter | solution.py:66
  832.6 42.2 %reduce-scatter.45.cloned.1.call-done = f32[320,128]{1,0:T(8,128)} async-done(((f32[320,1024]{1,0:T(8,128)}), f32[320,128]{1,0:T(8,128)}) %reduce-scatter.45.cloned.1.call-update) | async-done | bytes 163856 | tf_op jit(solution)/shard_map/reduce_scatter | solution.py:66
  876.3 42.0 %reduce-scatter.47.cloned.1.call-done = f32[320,128]{1,0:T(8,128)} async-done(((f32[320,1024]{1,0:T(8,128)}), f32[320,128]{1,0:T(8,128)}) %reduce-scatter.47.cloned.1.call-update) | async-done | bytes 163856 | tf_op jit(solution)/shard_map/reduce_scatter | solution.py:66
  (105 shorter events, 68.2 us)
Async XLA Ops:
  7.2 180.9 %copy-start = (bf16[320,3200]{1,0:T(8,128)(2,1)S(1)}, bf16[320,3200]{1,0:T(8,128)(2,1)}, u32[]{:S(2)}) copy-start(bf16[320,3200]{1,0:T(8,128)(2,1)} %param.29) | copy-start | bytes 6144004
  7.2 51.6 %all-gather.5.cloned.1.call-start = ((), (), s32[]{:S(2)}) async-start(), calls=%async_computation.16 | async-start | bytes 3481600 | tf_op jit(solution)/shard_map/all_gather | solution.py:54
  13.3 87.7 %all-gather.7.cloned.1.call-start = ((), (), s32[]{:S(2)}) async-start(), calls=%async_computation.19 | async-start | bytes 3481600 | tf_op jit(solution)/shard_map/all_gather | solution.py:54
  14.1 128.6 %all-gather.9.cloned.1.call-start = ((), (), s32[]{:S(2)}) async-start(), calls=%async_computation.22 | async-start | bytes 3481600 | tf_op jit(solution)/shard_map/all_gather | solution.py:54
  14.8 169.5 %all-gather.11.cloned.1.call-start = ((), (), s32[]{:S(2)}) async-start(), calls=%async_computation.25 | async-start | bytes 3481600 | tf_op jit(solution)/shard_map/all_gather | solution.py:54
  15.4 203.9 %reduce-scatter.27.cloned.1.call-start = ((), (), s32[]{:S(2)}) async-start(), calls=%async_computation.18 | async-start | bytes 294912 | tf_op jit(solution)/shard_map/reduce_scatter | solution.py:59
  62.5 198.0 %reduce-scatter.31.cloned.1.call-start = ((), (), s32[]{:S(2)}) async-start(), calls=%async_computation.21 | async-start | bytes 294912 | tf_op jit(solution)/shard_map/reduce_scatter | solution.py:59
  104.7 41.8 %copy-start.6 = (bf16[4,64,320]{2,1,0:T(8,128)(2,1)S(1)}, bf16[4,64,320]{2,1,0:T(8,128)(2,1)}, u32[]{:S(2)}) copy-start(bf16[4,64,320]{2,1,0:T(8,128)(2,1)} %param.27) | copy-start | bytes 491524
  104.8 196.8 %reduce-scatter.35.cloned.1.call-start = ((), (), s32[]{:S(2)}) async-start(), calls=%async_computation.24 | async-start | bytes 294912 | tf_op jit(solution)/shard_map/reduce_scatter | solution.py:59
  146.5 216.4 %reduce-scatter.49.cloned.1.call-start = ((), (), s32[]{:S(2)}) async-start(), calls=%async_computation.32 | async-start | bytes 557056
  148.9 272.0 %reduce-scatter.51.cloned.1.call-start = ((), (), s32[]{:S(2)}) async-start(), calls=%async_computation.33 | async-start | bytes 557056
  151.3 326.9 %reduce-scatter.53.cloned.1.call-start = ((), (), s32[]{:S(2)}) async-start(), calls=%async_computation.34 | async-start | bytes 557056
  153.8 382.2 %reduce-scatter.55.cloned.1.call-start = ((), (), s32[]{:S(2)}) async-start(), calls=%async_computation.35 | async-start | bytes 557056
  156.9 472.3 %reduce-scatter.39.cloned.1.call-start = ((), (), s32[]{:S(2)}) async-start(), calls=%async_computation.27 | async-start | bytes 294912 | tf_op jit(solution)/shard_map/reduce_scatter | solution.py:59
  188.0 502.5 %reduce-scatter.33.cloned.1.call-start = ((), (), s32[]{:S(2)}) async-start(), calls=%async_computation.23 | async-start | bytes 884736 | tf_op jit(solution)/shard_map/reduce_scatter | solution.py:58
  192.8 499.2 %reduce-scatter.29.cloned.1.call-start = ((), (), s32[]{:S(2)}) async-start(), calls=%async_computation.20 | async-start | bytes 884736 | tf_op jit(solution)/shard_map/reduce_scatter | solution.py:58
  197.6 503.7 %reduce-scatter.25.cloned.1.call-start = ((), (), s32[]{:S(2)}) async-start(), calls=%async_computation.17 | async-start | bytes 884736 | tf_op jit(solution)/shard_map/reduce_scatter | solution.py:58
  202.4 541.2 %reduce-scatter.37.cloned.1.call-start = ((), (), s32[]{:S(2)}) async-start(), calls=%async_computation.26 | async-start | bytes 884736 | tf_op jit(solution)/shard_map/reduce_scatter | solution.py:58
  207.2 580.3 %reduce-scatter.41.cloned.1.call-start = ((), (), s32[]{:S(2)}) async-start(), calls=%async_computation.28 | async-start | bytes 1474560 | tf_op jit(solution)/shard_map/reduce_scatter | solution.py:66
  245.7 585.3 %reduce-scatter.43.cloned.1.call-start = ((), (), s32[]{:S(2)}) async-start(), calls=%async_computation.29 | async-start | bytes 1474560 | tf_op jit(solution)/shard_map/reduce_scatter | solution.py:66
  261.2 69.3 %copy-start.7 = (s32[3]{0:T(128)S(1)}, s32[3]{0:T(128)}, u32[]{:S(2)}) copy-start(s32[3]{0:T(128)} %constant.202.clone.1) | copy-start | bytes 40
  286.8 587.9 %reduce-scatter.45.cloned.1.call-start = ((), (), s32[]{:S(2)}) async-start(), calls=%async_computation.30 | async-start | bytes 1474560 | tf_op jit(solution)/shard_map/reduce_scatter | solution.py:66
  328.0 590.3 %reduce-scatter.47.cloned.1.call-start = ((), (), s32[]{:S(2)}) async-start(), calls=%async_computation.31 | async-start | bytes 1474560 | tf_op jit(solution)/shard_map/reduce_scatter | solution.py:66
  673.8 3.1 copy-start.1
  673.8 6.2 copy-start.2
  680.0 3.6 copy-start.3
  683.6 3.7 copy-start.4
  919.8 0.8 copy-start.5
Sparse Core Ops, SparseCore 0:
  13.5 45.2 all-gather.4
  61.1 39.8 all-gather.6
  102.9 39.8 all-gather.8
  144.4 39.8 all-gather.10
  186.6 32.6 reduce-scatter.26
  221.8 38.5 reduce-scatter.30
  262.9 38.5 reduce-scatter.34
  304.7 58.0 reduce-scatter.48
  366.0 54.8 reduce-scatter.50
  423.4 54.7 reduce-scatter.52
  480.7 55.1 reduce-scatter.54
  538.5 36.1 reduce-scatter.38
  577.2 39.8 reduce-scatter.32
  619.6 39.5 reduce-scatter.28
  661.6 39.6 reduce-scatter.24
  703.9 39.6 reduce-scatter.36
  746.0 41.3 reduce-scatter.40
  789.9 41.1 reduce-scatter.42
  833.5 41.1 reduce-scatter.44
  877.1 41.1 reduce-scatter.46
where the time goes:
time: 933 us; the launch traced here: 927 us
  waiting for transfers between devices  606 us (65%)
  blocking collectives  206 us (22%)
  matrix products  65 us (7%)
  between operations  19.6 us (2%)
  other arithmetic  15.4 us (2%)
  local copies, waits for them, and re-layouts  14.7 us (2%)
    unnamed x24, waiting for transfers between devices  204 us
    reduce_scatter x4, waiting for transfers between devices, body(): lax.psum_scatter(grad_a_term, 'row', scatter_dimension=1, tiled=True)  168 us
    all_gather x4, waiting for transfers between devices, body(): piece = lax.all_gather(upstream, 'col', axis=0, tiled=True)  144 us
    all_gather x4, blocking collectives, body(): factor_full = lax.all_gather(factor_grad, 'col', axis=1, tiled=True)  114 us
    all_gather x4, blocking collectives, body(): hidden_all = lax.all_gather(hidden, 'row', axis=0, tiled=True)  92.3 us
    reduce_scatter x4, waiting for transfers between devices, body(): lax.psum_scatter(main_terms, 'row', scatter_dimension=0, tiled=True)  48.7 us
    reduce_scatter x4, waiting for transfers between devices, body(): lax.psum_scatter(side_terms, 'row', scatter_dimension=0, tiled=True)  41.4 us
    dot_general x12, matrix products, contract_cols(): lax.dot_general(left, right, (((1,), (1,)), ((), ())), preferred_element_...  39.4 us
  transfers between devices with their start and end apart: 20, of which 17 were waited for; matrix products, arithmetic and copies ran while one was open for 9% of the time, Pallas kernels for 0%

commit v1 on v0

v1 whole, which is shorter than its diff:
```python
import jax
import jax.numpy as jnp
from jax import lax
from jax.experimental import pallas as pl
from jax.experimental.pallas import tpu as pltpu
from jax.sharding import PartitionSpec as P

ROWS = 8
PLANES = 8
SLOTS = 4
CHAINS = 2
F32 = jnp.float32
BF16 = jnp.bfloat16
RING = [(c, (c + 2) % 16) if c % 2 == 0 else (c, (c - 2) % 16) for c in range(16)]
SWAP = [(c, c ^ 1) for c in range(16)]
SAME_CORE = [list(range(0, 16, 2)), list(range(1, 16, 2))]
SMEM = pl.BlockSpec(memory_space=pltpu.SMEM)
VMEM = pl.BlockSpec(memory_space=pltpu.VMEM)
ANY = pl.BlockSpec(memory_space=pl.ANY)
MIB = 1024 * 1024
GUESS = pl.CostEstimate(flops=3 * 10**9, bytes_accessed=8 * MIB, transcendentals=0)


def dot_last(left, right):
    return lax.dot_general(
        left, right, (((1,), (1,)), ((), ())), preferred_element_type=F32
    )


def dot_first(left, right):
    return lax.dot_general(
        left, right, (((0,), (0,)), ((), ())), preferred_element_type=F32
    )


def origin_of(place, step):
    return lax.rem(place[0] + (2 * place[1] - 1) * step + PLANES, PLANES)


def keep_kernel(*refs):
    sems, refs = refs[-1], refs[:-1]
    count = len(refs) // 2
    copies = [
        pltpu.make_async_copy(refs[n], refs[count + n], sems.at[n]) for n in range(count)
    ]
    for copy in copies:
        copy.start()
    for copy in copies:
        copy.wait()


def kept_in_vmem(arrays):
    return pl.pallas_call(
        keep_kernel,
        out_shape=tuple(pltpu.VMEM(array.shape, array.dtype) for array in arrays),
        in_specs=[ANY] * len(arrays),
        out_specs=(VMEM,) * len(arrays),
        scratch_shapes=[pltpu.SemaphoreType.DMA((len(arrays),))],
        compiler_params=pltpu.CompilerParams(vmem_limit_bytes=24 * MIB),
        cost_estimate=GUESS,
    )(*arrays)


def step_kernel(steps, place, *refs):
    count = CHAINS * len(steps)
    units, weights = refs[:count], refs[count : count + 4]
    main_out, side_out, acc_c, acc_d, main, side, sems = refs[-7:]
    height = units[0].shape[1]
    rows = jnp.concatenate(
        [unit[n] for unit in units for n in range(SLOTS // CHAINS)], axis=0
    )
    acc_a = dot_last(rows, weights[0][...])
    acc_b = dot_last(rows, weights[1][...])
    for at in range(len(steps)):
        for slot in range(SLOTS):
            top = height * (SLOTS * at + slot)
            here = slice(top, top + height)
            both = jnp.concatenate([acc_a[here], acc_b[here]], axis=1)
            main[at, slot] = both.astype(BF16)
    copies = [
        pltpu.make_async_copy(
            main.at[at], main_out.at[origin_of(place, step)], sems.at[2 * at]
        )
        for at, step in enumerate(steps)
    ]
    for copy in copies:
        copy.start()
    acc_c[...] = dot_last(rows, weights[2][...])
    acc_d[...] = dot_last(rows, weights[3][...])
    half = acc_c.shape[1] // SLOTS
    for at, step in enumerate(steps):
        for slot in range(SLOTS):
            top = height * (SLOTS * at + slot)
            here = slice(top, top + height)
            entry = place[2 + slot]
            lanes = pl.ds(pl.multiple_of(entry // 2 * 2 * half, 2 * half), 2 * half)
            parts = []
            for acc in (acc_c, acc_d):
                pair = acc[here, lanes]
                parts.append(jnp.where(entry % 2 == 0, pair[:, :half], pair[:, half:]))
            side[at, slot] = jnp.concatenate(parts, axis=1).astype(BF16)
        copy = pltpu.make_async_copy(
            side.at[at], side_out.at[origin_of(place, step)], sems.at[1 + 2 * at]
        )
        copy.start()
        copies.append(copy)
    for copy in copies:
        copy.wait()


def step_products(steps, place, units, weights, done):
    height = units[0].shape[1]
    feats, ranks = weights[0].shape[0], weights[2].shape[0]
    count = len(units)
    rows = SLOTS * len(steps) * height
    main_shape = (SLOTS, height, 2 * feats)
    side_shape = (SLOTS, height, 2 * ranks // SLOTS)

    def kernel(*refs):
        step_kernel(steps, *refs)

    return pl.pallas_call(
        kernel,
        out_shape=(
            jax.ShapeDtypeStruct((ROWS,) + main_shape, BF16),
            jax.ShapeDtypeStruct((ROWS,) + side_shape, BF16),
        ),
        in_specs=[SMEM] + [VMEM] * (count + 4) + [ANY] * len(done),
        out_specs=(ANY, ANY),
        scratch_shapes=[
            pltpu.VMEM((rows, ranks), F32),
            pltpu.VMEM((rows, ranks), F32),
            pltpu.VMEM((len(steps),) + main_shape, BF16),
            pltpu.VMEM((len(steps),) + side_shape, BF16),
            pltpu.SemaphoreType.DMA((2 * len(steps),)),
        ],
        input_output_aliases={count + 5: 0, count + 6: 1} if done else {},
        compiler_params=pltpu.CompilerParams(vmem_limit_bytes=24 * MIB),
        cost_estimate=GUESS,
    )(place, *units, *weights, *done)


def small_call(kernel, out_shape, args, scratch=(), limit=24):
    scalars = sum(arg.ndim == 1 for arg in args)
    return pl.pallas_call(
        kernel,
        out_shape=out_shape,
        in_specs=[SMEM] * scalars + [VMEM] * (len(args) - scalars),
        out_specs=jax.tree.map(lambda _: VMEM if not scratch else ANY, out_shape),
        scratch_shapes=list(scratch),
        compiler_params=pltpu.CompilerParams(vmem_limit_bytes=limit * MIB),
        cost_estimate=GUESS,
    )(*args)


def pick(place, low, high):
    first = place[1] == 0
    return jnp.where(first, low, high), jnp.where(first, high, low)


def own_rows(place, height):
    start = pl.multiple_of(place[1] * height, height)
    return pl.ds(start, height)


def other_rows(place, height):
    start = pl.multiple_of((1 - place[1]) * height, height)
    return pl.ds(start, height)


def masked_sum(place, terms, slot):
    total = terms[0, slot].astype(F32)
    for source in range(1, ROWS):
        total = total + terms[source, slot].astype(F32)
    height = total.shape[0]
    start = 2 * height * place[6] + height * place[1]
    position = start + lax.broadcasted_iota(jnp.int32, total.shape, 0)
    return jnp.where(position < place[7 + slot], total, 0.0)


def send_to_all(stage, out, sems):
    copies = [pltpu.make_async_copy(stage, out.at[n], sems.at[n]) for n in range(8)]
    for copy in copies:
        copy.start()
    for copy in copies:
        copy.wait()


def hidden_kernel(place, x, lefts, keep, give):
    height, width = keep.shape[2:]
    for slot in range(SLOTS):
        both = jnp.dot(x[slot], lefts[place[2 + slot]], preferred_element_type=F32)
        mine, others = pick(place, both[:height], both[height:])
        for plane in range(PLANES):
            lanes = slice(width * plane, width * (plane + 1))
            keep[plane, slot] = mine[:, lanes]
            give[plane, slot] = others[:, lanes]


def share_kernel(place, terms, x, out, stage, sems):
    for slot in range(SLOTS):
        hidden = masked_sum(place, terms, slot).astype(BF16)
        half = hidden.shape[1] // 2
        stacked = jnp.concatenate([hidden[:, :half], hidden[:, half:]], axis=0)
        stage[slot] = jnp.concatenate([x[slot], stacked], axis=1)
    send_to_all(stage, out, sems)


def factor_kernel(place, terms, out):
    for slot in range(SLOTS):
        total = masked_sum(place, terms, slot)
        half = total.shape[1] // 2
        turned = jnp.concatenate([total[:, half:], total[:, :half]], axis=1)
        out[slot] = jnp.where(place[1] == 0, total, turned).astype(BF16)


def stack_kernel(place, *refs):
    pieces, (out, sems) = refs[:PLANES], refs[PLANES:]
    copies = []
    for hop, piece in enumerate(pieces):
        origin = lax.rem(place[0] - hop + PLANES, PLANES)
        copies.append(pltpu.make_async_copy(piece, out.at[origin], sems.at[hop]))
    for copy in copies:
        copy.start()
    for copy in copies:
        copy.wait()


def main_kernel(place, terms, keep, give):
    feats = keep.shape[-1]
    for slot in range(SLOTS):
        total = masked_sum(place, terms, slot)
        keep[slot] = total[:, :feats]
        give[slot] = total[:, feats:]


def grad_in_kernel(place, mine, others, keep, got, lefts, out):
    height = keep.shape[1]
    for slot in range(SLOTS):
        rows = jnp.concatenate(
            [
                jnp.concatenate([part[plane, slot] for plane in range(PLANES)], axis=1)
                for part in (mine, others)
            ],
            axis=0,
        )
        side = dot_last(rows, lefts[place[2 + slot]])
        out[slot, own_rows(place, height)] = (keep[slot] + side[:height]).astype(BF16)
        out[slot, other_rows(place, height)] = (got[slot] + side[height:]).astype(BF16)


def grad_a_kernel(place, scales, mine, others, shared, out):
    height = mine.shape[2]
    feats = out.shape[1]
    for slot in range(SLOTS):
        acts, factors = [], []
        for part, here in (
            (mine, own_rows(place, height)),
            (others, other_rows(place, height)),
        ):
            for row in range(ROWS):
                acts.append(shared[row, slot, here, :feats])
                factors.append(part[row, slot])
        acts = jnp.concatenate(acts, axis=0)
        factors = jnp.concatenate(factors, axis=0)
        out[place[2 + slot]] = dot_first(acts, factors) * scales[slot]


def grad_b_kernel(place, scales, shared, *refs):
    units, (keep, give, rows, sems) = refs[:-4], refs[-4:]
    ranks = keep.shape[1]
    height = units[0].shape[1]
    feats = shared.shape[-1] - ranks
    loads = []
    for slot in range(SLOTS):
        for step in range(PLANES):
            here = pl.ds(height * step, height)
            pair = SLOTS // CHAINS
            unit = units[CHAINS * step + slot // pair].at[slot % pair]
            sem = sems.at[PLANES * slot + step]
            loads.append(pltpu.make_async_copy(unit, rows.at[slot, here], sem))
    for load in loads:
        load.start()
    for slot in range(SLOTS):
        hidden = []
        for step in range(PLANES):
            origin = origin_of(place, step)
            pair = [
                shared[origin, slot, here, feats:]
                for here in (own_rows(place, height), other_rows(place, height))
            ]
            hidden.append(jnp.concatenate(pair, axis=1))
            loads[PLANES * slot + step].wait()
        both = dot_first(jnp.concatenate(hidden, axis=0), rows[slot]) * scales[slot]
        entry = place[2 + slot]
        keep[entry] = both[:ranks]
        give[entry] = both[ranks:]


def grad_b_parts(place, scales, shared, units):
    height, depth = units[0].shape[1:]
    ranks = shared.shape[2]
    part = jax.ShapeDtypeStruct((SLOTS, ranks, depth), F32)
    return pl.pallas_call(
        grad_b_kernel,
        out_shape=(part, part),
        in_specs=[SMEM, SMEM, VMEM] + [ANY] * len(units),
        out_specs=(VMEM, VMEM),
        scratch_shapes=[
            pltpu.VMEM((SLOTS, PLANES * height, depth), BF16),
            pltpu.SemaphoreType.DMA((SLOTS * PLANES,)),
        ],
        compiler_params=pltpu.CompilerParams(vmem_limit_bytes=60 * MIB),
        cost_estimate=GUESS,
    )(place, scales, shared, *units)


def body(x, dy, weight, lefts, rights, chosen, counts):
    slots, tokens, feats = x.shape
    height, depth = dy.shape[1:]
    ranks = rights.shape[1]
    col = lax.axis_index("col")
    row = lax.axis_index("row")
    plane, core = col // 2, col % 2

    def swap(piece):
        return lax.ppermute(piece, "col", SWAP)

    def over_planes(pieces):
        return lax.all_to_all(pieces, "col", 0, 0, axis_index_groups=SAME_CORE)

    def over_rows(pieces):
        return lax.all_to_all(pieces, "row", 0, 0)

    def after(value, *earlier):
        return lax.optimization_barrier((value,) + earlier)[0]

    def passed_on(units):
        return [lax.ppermute(unit, "col", RING) for unit in units]

    shape = jax.ShapeDtypeStruct
    sems = pltpu.SemaphoreType.DMA((8,))
    entry = chosen - lax.axis_index("trial") * slots
    scales = lax.rsqrt(counts.astype(F32))
    place = jnp.concatenate([jnp.stack([plane, core]), entry, row[None], counts])
    place = place.astype(jnp.int32)

    pair = slots // CHAINS
    own = [[dy[pair * n : pair * (n + 1)] for n in range(CHAINS)]]
    own.append(passed_on(own[0]))
    ups = after(rights.reshape(slots * ranks, depth), *own[1])
    weight = after(weight, *own[1])
    weights = [weight, swap(weight), ups, swap(ups)]
    own.append(passed_on(own[1]))

    piece = (PLANES, slots, height, 2 * ranks)
    keep, give = small_call(
        hidden_kernel,
        (shape(piece, F32), shape(piece, F32)),
        (place, after(x, own[1][0]), lefts),
    )
    terms = over_planes((keep + swap(give)).astype(BF16))
    own.append(passed_on(own[2]))
    weights = kept_in_vmem(weights)
    products = step_products((0, 1), place, own[0] + own[1], weights, ())
    own[3][0] = after(own[3][0], *products)
    own.append(passed_on(own[3]))
    wide = (slots, tokens, feats + ranks)
    shared = small_call(
        share_kernel,
        shape((ROWS,) + wide, BF16),
        (place, terms, x),
        scratch=(pltpu.VMEM(wide, BF16), sems),
    )
    shared = over_rows(shared)
    own.append(passed_on(own[4]))
    products = step_products((2, 3), place, own[2] + own[3], weights, products)
    own[5][0] = after(own[5][0], *products)
    own.append(passed_on(own[5]))
    products = step_products((4, 5), place, own[4] + own[5], weights, products)
    own[6][1] = after(own[6][1], *products)
    own.append(passed_on(own[6]))
    products = step_products((6, 7), place, own[6] + own[7], weights, products)
    main_parts, side_parts = products

    side_terms = over_rows(after(side_parts, shared))
    keep_b, give_b = grad_b_parts(place, scales, after(shared, side_parts), sum(own, []))
    main_terms = over_rows(after(main_parts, side_terms))
    factor = small_call(
        factor_kernel, shape(piece[1:], BF16), (place, after(side_terms, keep_b))
    )
    got_b = swap(after(give_b, factor))
    hops = [factor] + [
        lax.ppermute(factor, "col", [(c, (c + 2 * hop) % 16) for c in range(16)])
        for hop in range(1, PLANES)
    ]
    hops[-1] = after(hops[-1], main_terms)
    factor_planes = small_call(
        stack_kernel, shape(piece, BF16), (place, *hops), scratch=(sems,)
    )

    part = (slots, height, feats)
    keep, give = small_call(
        main_kernel, (shape(part, F32), shape(part, F32)), (place, main_terms)
    )
    factor_tokens = over_rows(factor_planes)
    grad_in = small_call(
        grad_in_kernel,
        shape(x.shape, BF16),
        (place, factor_planes, swap(factor_planes), keep, swap(give), lefts),
    )
    grad_b = keep_b + got_b
    grad_a = small_call(
        grad_a_kernel,
        shape((slots, feats, 2 * ranks), F32),
        (place, scales, factor_tokens, swap(factor_tokens), shared),
    )
    return grad_in, grad_a, grad_b


def solution(mesh):
    return jax.shard_map(
        body,
        mesh=mesh,
        in_specs=(
            P("trial", "row", "col"),
            P("trial", "col", "row"),
            P("col", "row"),
            P("trial", "col", None),
            P("trial", "col", "row"),
            P("trial"),
            P("trial"),
        ),
        out_specs=(P("trial", "row", "col"), P("trial", "col", "row"), P("trial", "col", "row")),
        check_vma=False,
    )
```

time: 933 us -> 173 us (0.19)
  waiting for transfers between devices: 606 us -> 38.3 us
  blocking collectives: 206 us -> 0 us
  starting transfers between devices: 0.82 us -> 72.7 us
  matrix products: 65 us -> 0 us
  Pallas kernels: 0 us -> 40.9 us
  between operations: 19.6 us -> 1.1 us
  other arithmetic: 15.4 us -> 5.5 us
    reduce_scatter x12 -> x0, waiting for transfers between devices: 258 us -> none  [the longest x4 168 us: body(): lax.psum_scatter(grad_a_term, 'row', scatter_dimension=1, tiled=True)]
    all_gather x8 -> x0, blocking collectives: 206 us -> none  [the longest x4 114 us: body(): factor_full = lax.all_gather(factor_grad, 'col', axis=1, tiled=True)]
    unnamed x24 -> x0, waiting for transfers between devices: 204 us -> none
    all_gather x4 -> x0, waiting for transfers between devices: 144 us -> none  [body(): piece = lax.all_gather(upstream, 'col', axis=0, tiled=True)]
    dot_general x24 -> x0, matrix products: 65 us -> none  [the longest x12 39.4 us: contract_cols(): lax.dot_general(left, right, (((1,), (1,)), ((), ())), preferred_element_...]
    ppermute x0 -> x28, starting transfers between devices: none -> 48 us  [the longest x14 27.5 us: passed_on(): return [lax.ppermute(unit, 'col', RING) for unit in units]]
    pallas_call x0 -> x13, Pallas kernels: none -> 40.9 us  [the longest x4 18.2 us: step_products(): pl.pallas_call(kernel, out_shape=(jax.ShapeDtypeStruct((ROWS,) + main_sha...]
    ppermute x0 -> x28, waiting for transfers between devices: none -> 24.8 us  [the longest x14 24.7 us: passed_on(): return [lax.ppermute(unit, 'col', RING) for unit in units]]
  transfers between devices with their start and end apart: 20 -> 33, of which waited for: 17 -> 10; matrix products, arithmetic and copies ran while one was open for 9% -> 1% of each run, Pallas kernels for 0% -> 23%
where the time goes in v1:
time: 173 us; the launch traced here: 172 us
  starting transfers between devices  72.7 us (42%)
  Pallas kernels  40.9 us (24%)
  waiting for transfers between devices  38.3 us (22%)
  local copies, waits for them, and re-layouts  13.2 us (8%)
  other arithmetic  5.5 us (3%)
    ppermute x14, starting transfers between devices, passed_on(): return [lax.ppermute(unit, 'col', RING) for unit in units]  27.5 us
    ppermute x14, waiting for transfers between devices, passed_on(): return [lax.ppermute(unit, 'col', RING) for unit in units]  24.7 us
    all_to_all x4, starting transfers between devices, over_rows(): return lax.all_to_all(pieces, 'row', 0, 0)  19.1 us
    pallas_call x4, Pallas kernels, step_products(): pl.pallas_call(kernel, out_shape=(jax.ShapeDtypeStruct((ROWS,) + main_sha...  18.2 us
    all_to_all x4, waiting for transfers between devices, over_rows(): return lax.all_to_all(pieces, 'row', 0, 0)  13.5 us
    unnamed x68, local copies, waits for them, and re-layouts  11.9 us
    ppermute x7, starting transfers between devices, swap(): return lax.ppermute(piece, 'col', SWAP)  10.9 us
    pallas_call x7, Pallas kernels, small_call(): pl.pallas_call(kernel, out_shape=out_shape, in_specs=[SMEM] * scalars + [...  10.5 us
  transfers between devices with their start and end apart: 33, of which 10 were waited for; matrix products, arithmetic and copies ran while one was open for 1% of the time, Pallas kernels for 23%

profile of v1, /device:TPU:1, one launch (start us, length us, event | category | flops | bytes accessed | tf_op | source)
XLA Modules:
  0.0 171.7 jit_solution(5103994221540391266)
XLA Ops:
  1.9 6.5 %collective-permute-start = (bf16[2,32,3200]{2,1,0:T(8,128)(2,1)S(1)}, bf16[2,32,3200]{2,1,0:T(8,128)(2,1)S(1)}, u32[]{:S(2)}, u32[]{:S(2)}) collective-permute-start(bf16[2,32,3200]{2,1,0:T(8,128)(2,1)S(1)} %get-tuple-element.64.refs_1_.refs_0_), channel_id=1, source_target_pairs={{0,2},{1,15},{2,4},{3,1},{4,6},{5,3},{6,8},{7,5},{8,10},{9,7},{10,... | collective-permute-start | bytes 1228808 | tf_op jit(solution)/shard_map/ppermute | solution.py:339
  9.1 4.2 %collective-permute-done.refs_3_.refs_2_ = bf16[2,32,3200]{2,1,0:T(8,128)(2,1)S(1)} collective-permute-done((bf16[2,32,3200]{2,1,0:T(8,128)(2,1)S(1)}, bf16[2,32,3200]{2,1,0:T(8,128)(2,1)S(1)}, u32[]{:S(2)}, u32[]{:S(2)}) %collective-permute-start) | collective-permute-done | bytes 409632 | tf_op jit(solution)/shard_map/ppermute | solution.py:339
  13.3 4.4 %collective-permute-done.3.refs_4_.refs_3_ = bf16[2,32,3200]{2,1,0:T(8,128)(2,1)S(1)} collective-permute-done((bf16[2,32,3200]{2,1,0:T(8,128)(2,1)S(1)}, bf16[2,32,3200]{2,1,0:T(8,128)(2,1)S(1)}, u32[]{:S(2)}, u32[]{:S(2)}) %collective-permute-start.3) | collective-permute-done | bytes 409632 | tf_op jit(solution)/shard_map/ppermute | solution.py:339
  17.7 2.0 %collective-permute-start.4 = (bf16[320,3200]{1,0:T(8,128)(2,1)}, bf16[320,3200]{1,0:T(8,128)(2,1)}, u32[]{:S(2)}, u32[]{:S(2)}) collective-permute-start(bf16[320,3200]{1,0:T(8,128)(2,1)} %refs_0_), channel_id=1, source_target_pairs={{0,1},{1,0},{2,3},{3,2},{4,5},{5,4},{6,7},{7,6},{8,9},{9,8},{10,11... | collective-permute-start | bytes 6144008 | tf_op jit(solution)/shard_map/ppermute | solution.py:327
  26.9 2.7 %collective-permute-start.9 = (bf16[2,32,3200]{2,1,0:T(8,128)(2,1)S(1)}, bf16[2,32,3200]{2,1,0:T(8,128)(2,1)S(1)}, u32[]{:S(2)}, u32[]{:S(2)}) collective-permute-start(bf16[2,32,3200]{2,1,0:T(8,128)(2,1)S(1)} %collective-permute-done.8.refs_2_.refs_5_), channel_id=1, source_target_pairs={{0,2},{1,15},{2,4},{3,1},{4,6},{5,3},{6,8},{7,5},{8,10},{9,7},{10,... | collective-permute-start | bytes 1228808 | tf_op jit(solution)/shard_map/ppermute | solution.py:339
  29.6 2.2 %collective-permute-done.1.refs_1_.refs_4_ = bf16[2,32,3200]{2,1,0:T(8,128)(2,1)S(1)} collective-permute-done((bf16[2,32,3200]{2,1,0:T(8,128)(2,1)S(1)}, bf16[2,32,3200]{2,1,0:T(8,128)(2,1)S(1)}, u32[]{:S(2)}, u32[]{:S(2)}) %collective-permute-start.1) | collective-permute-done | bytes 409632 | tf_op jit(solution)/shard_map/ppermute | solution.py:339
  31.7 2.5 %collective-permute-start.2 = (bf16[2,32,3200]{2,1,0:T(8,128)(2,1)S(1)}, bf16[2,32,3200]{2,1,0:T(8,128)(2,1)}, u32[]{:S(2)}, u32[]{:S(2)}) collective-permute-start(bf16[2,32,3200]{2,1,0:T(8,128)(2,1)S(1)} %collective-permute-done.1.refs_1_.refs_4_), channel_id=1, source_target_pairs={{0,2},{1,15},{2,4},{3,1},{4,6},{5,3},{6,8},{7,5},{8,10},{9,7},{10,... | collective-permute-start | bytes 1228808 | tf_op jit(solution)/shard_map/ppermute | solution.py:339
  35.1 5.5 %all-to-all-start = ((bf16[8,4,32,128]{3,2,1,0:T(8,128)(2,1)}), bf16[8,4,32,128]{3,2,1,0:T(8,128)(2,1)S(1)}, u32[]{:S(2)}, u32[]{:S(2)}) async-start(bf16[8,4,32,128]{3,2,1,0:T(8,128)(2,1)} %add_convert_fusion), calls=%async_computation | async-start | bytes 524288 | tf_op jit(solution)/shard_map/all_to_all | solution.py:330
  40.7 2.7 %collective-permute-start.11 = (bf16[2,32,3200]{2,1,0:T(8,128)(2,1)S(1)}, bf16[2,32,3200]{2,1,0:T(8,128)(2,1)}, u32[]{:S(2)}, u32[]{:S(2)}) collective-permute-start(bf16[2,32,3200]{2,1,0:T(8,128)(2,1)S(1)} %collective-permute-done.9.refs_4_.refs_7_), channel_id=1, source_target_pairs={{0,2},{1,15},{2,4},{3,1},{4,6},{5,3},{6,8},{7,5},{8,10},{9,7},{10,... | collective-permute-start | bytes 1228808 | tf_op jit(solution)/shard_map/ppermute | solution.py:339
  45.0 3.0 %shard_map.94 = (bf16[320,3200]{1,0:T(8,128)(2,1)S(1)}, bf16[320,3200]{1,0:T(8,128)(2,1)S(1)}, bf16[256,3200]{1,0:T(8,128)(2,1)S(1)}, bf16[256,3200]{1,0:T(8,128)(2,1)S(1)}) custom-call(bf16[320,3200]{1,0:T(8,128)(2,1)S(1)} %copy-done.8, bf16[320,3200]{1,0:T(8,128)(2,1)} %collective-permute-done.4.refs_1_, bf16[256,3200]{1,0:T(8,128)(2,1)} %bitcast.3.refs_2_, ...), custom_call_target="tpu_custom_call" | custom-call | flops 3000000000 | bytes 8388608 | tf_op jit(solution)/shard_map/pallas_call | solution.py:53
  48.1 4.2 %shard_map.95 = (bf16[8,4,32,640]{3,2,1,0:T(8,128)(2,1)}, bf16[8,4,32,128]{3,2,1,0:T(8,128)(2,1)}) custom-call(s32[11]{0:T(128)S(1)} %concatenate.3.refs_0_.place, bf16[2,32,3200]{2,1,0:T(8,128)(2,1)S(1)} %get-tuple-element.64.refs_1_.refs_0_, bf16[2,32,3200]{2,1,0:T(8,128)(2,1)S(1)} %get-tuple-element.63.refs_2_.refs_1_, ...), custom_call_target="tpu_custom_call" | custom-call | flops 3000000000 | bytes 8388608 | tf_op jit(solution)/shard_map/pallas_call | solution.py:122
  54.8 5.0 %collective-permute-done.6.refs_1_.refs_8_ = bf16[2,32,3200]{2,1,0:T(8,128)(2,1)} collective-permute-done((bf16[2,32,3200]{2,1,0:T(8,128)(2,1)}, bf16[2,32,3200]{2,1,0:T(8,128)(2,1)}, u32[]{:S(2)}, u32[]{:S(2)}) %collective-permute-start.6) | collective-permute-done | bytes 409632 | tf_op jit(solution)/shard_map/ppermute | solution.py:339
  59.9 2.1 %collective-permute-start.7 = (bf16[2,32,3200]{2,1,0:T(8,128)(2,1)}, bf16[2,32,3200]{2,1,0:T(8,128)(2,1)}, u32[]{:S(2)}, u32[]{:S(2)}) collective-permute-start(bf16[2,32,3200]{2,1,0:T(8,128)(2,1)} %collective-permute-done.6.refs_1_.refs_8_), channel_id=1, source_target_pairs={{0,2},{1,15},{2,4},{3,1},{4,6},{5,3},{6,8},{7,5},{8,10},{9,7},{10,... | collective-permute-start | bytes 1228808 | tf_op jit(solution)/shard_map/ppermute | solution.py:339
  63.9 5.2 %all-to-all-start.1 = ((bf16[8,4,64,384]{3,2,1,0:T(8,128)(2,1)}), bf16[8,4,64,384]{3,2,1,0:T(8,128)(2,1)S(1)}, u32[]{:S(2)}, u32[]{:S(2)}) async-start(bf16[8,4,64,384]{3,2,1,0:T(8,128)(2,1)} %shard_map.100), calls=%async_computation.1 | async-start | bytes 3145728 | tf_op jit(solution)/shard_map/all_to_all | solution.py:333
  75.5 4.7 %shard_map.96 = (bf16[8,4,32,640]{3,2,1,0:T(8,128)(2,1)}, bf16[8,4,32,128]{3,2,1,0:T(8,128)(2,1)}) custom-call(s32[11]{0:T(128)S(1)} %concatenate.3.refs_0_.place, bf16[2,32,3200]{2,1,0:T(8,128)(2,1)S(1)} %copy-done.14, bf16[2,32,3200]{2,1,0:T(8,128)(2,1)S(1)} %copy-done.12, ...), custom_call_target="tpu_custom_call", output_to_operand_aliasing={{0}: (9, {}), {1}: (10, {})} | custom-call | flops 3000000000 | bytes 8388608 | tf_op jit(solution)/shard_map/pallas_call | solution.py:122
  81.4 5.0 %shard_map.97 = (bf16[8,4,32,640]{3,2,1,0:T(8,128)(2,1)}, bf16[8,4,32,128]{3,2,1,0:T(8,128)(2,1)}) custom-call(s32[11]{0:T(128)S(1)} %concatenate.3.refs_0_.place, bf16[2,32,3200]{2,1,0:T(8,128)(2,1)} %collective-permute-done.6.refs_1_.refs_8_, ...), custom_call_target="tpu_custom_call", output_to_operand_aliasing={{0}: (9, {}), {1}: (10, {})} | custom-call | flops 3000000000 | bytes 8388608 | tf_op jit(solution)/shard_map/pallas_call | solution.py:122
  87.6 2.4 %collective-permute-start.14 = (bf16[2,32,3200]{2,1,0:T(8,128)(2,1)S(1)}, bf16[2,32,3200]{2,1,0:T(8,128)(2,1)S(1)}, u32[]{:S(2)}, u32[]{:S(2)}) collective-permute-start(bf16[2,32,3200]{2,1,0:T(8,128)(2,1)S(1)} %collective-permute-done.10.refs_1_.refs_12_), channel_id=1, source_target_pairs={{0,2},{1,15},{2,4},{3,1},{4,6},{5,3},{6,8},{7,5},{8,10},{9,7},{10,... | collective-permute-start | bytes 1228808 | tf_op jit(solution)/shard_map/ppermute | solution.py:339
  90.5 2.9 %collective-permute-done.15.refs_4_.refs_15_ = bf16[2,32,3200]{2,1,0:T(8,128)(2,1)S(1)} collective-permute-done((bf16[2,32,3200]{2,1,0:T(8,128)(2,1)S(1)}, bf16[2,32,3200]{2,1,0:T(8,128)(2,1)S(1)}, u32[]{:S(2)}, u32[]{:S(2)}) %collective-permute-start.15) | collective-permute-done | bytes 409632 | tf_op jit(solution)/shard_map/ppermute | solution.py:339
  93.4 4.7 %collective-permute-done.14.refs_3_.refs_14_ = bf16[2,32,3200]{2,1,0:T(8,128)(2,1)S(1)} collective-permute-done((bf16[2,32,3200]{2,1,0:T(8,128)(2,1)S(1)}, bf16[2,32,3200]{2,1,0:T(8,128)(2,1)S(1)}, u32[]{:S(2)}, u32[]{:S(2)}) %collective-permute-start.14) | collective-permute-done | bytes 409632 | tf_op jit(solution)/shard_map/ppermute | solution.py:339
  98.1 4.3 %shard_map.98 = (bf16[8,4,32,640]{3,2,1,0:T(8,128)(2,1)}, bf16[8,4,32,128]{3,2,1,0:T(8,128)(2,1)}) custom-call(s32[11]{0:T(128)S(1)} %concatenate.3.refs_0_.place, bf16[2,32,3200]{2,1,0:T(8,128)(2,1)S(1)} %collective-permute-done.10.refs_1_.refs_12_, ...), custom_call_target="tpu_custom_call", output_to_operand_aliasing={{0}: (9, {}), {1}: (10, {})} | custom-call | flops 3000000000 | bytes 8388608 | tf_op jit(solution)/shard_map/pallas_call | solution.py:122
  103.1 5.1 %all-to-all-start.2 = ((bf16[8,4,32,128]{3,2,1,0:T(8,128)(2,1)}), bf16[8,4,32,128]{3,2,1,0:T(8,128)(2,1)S(1)}, u32[]{:S(2)}, u32[]{:S(2)}) async-start(bf16[8,4,32,128]{3,2,1,0:T(8,128)(2,1)} %get-tuple-element.52), calls=%async_computation.2 | async-start | bytes 524288 | tf_op jit(solution)/shard_map/all_to_all | solution.py:333
  108.2 9.2 %shard_map.101 = (f32[4,64,3200]{2,1,0:T(8,128)}, f32[4,64,3200]{2,1,0:T(8,128)}) custom-call(s32[11]{0:T(128)} %copy-done.4, f32[4]{0:T(128)} %convert_rsqrt_fusion.scales, bf16[8,4,64,384]{3,2,1,0:T(8,128)(2,1)} %copy-done, bf16[2,32,3200]{2,1,0:T(8,128)(2,1)} %copy-done.3, bf16[2,32,3200]{2,1,0:T(8,128)(2,1)} %copy-done.2, ...), custom_call_target="tpu_custom_call" | custom-call | flops 3000000000 | bytes 8388608 | tf_op jit(solution)/shard_map/pallas_call | solution.py:304
  118.2 5.9 %collective-permute-start.27 = (f32[4,64,3200]{2,1,0:T(8,128)}, f32[4,64,3200]{2,1,0:T(8,128)}, u32[]{:S(2)}, u32[]{:S(2)}) collective-permute-start(f32[4,64,3200]{2,1,0:T(8,128)} %get-tuple-element.62), channel_id=1, source_target_pairs={{0,1},{1,0},{2,3},{3,2},{4,5},{5,4},{6,7},{7,6},{8,9},{9,8},{10,11... | collective-permute-start | bytes 9830408 | tf_op jit(solution)/shard_map/ppermute | solution.py:327
  124.1 5.4 %all-to-all-start.3 = ((bf16[8,4,32,640]{3,2,1,0:T(8,128)(2,1)}), bf16[8,4,32,640]{3,2,1,0:T(8,128)(2,1)S(1)}, u32[]{:S(2)}, u32[]{:S(2)}) async-start(bf16[8,4,32,640]{3,2,1,0:T(8,128)(2,1)} %get-tuple-element.57), calls=%async_computation.3 | async-start | bytes 2621440 | tf_op jit(solution)/shard_map/all_to_all | solution.py:333
  132.4 4.2 %collective-permute-start.20 = (bf16[4,32,128]{2,1,0:T(8,128)(2,1)S(1)}, bf16[4,32,128]{2,1,0:T(8,128)(2,1)S(1)}, u32[]{:S(2)}, u32[]{:S(2)}) collective-permute-start(bf16[4,32,128]{2,1,0:T(8,128)(2,1)S(1)} %shard_map.102.refs_0_), channel_id=1, source_target_pairs={{0,8},{1,9},{2,10},{3,11},{4,12},{5,13},{6,14},{7,15},{8,0},{9,1},... | collective-permute-start | bytes 98312 | tf_op jit(solution)/shard_map/ppermute | solution.py:394
  136.7 2.4 %collective-permute-start.22 = (bf16[4,32,128]{2,1,0:T(8,128)(2,1)S(1)}, bf16[4,32,128]{2,1,0:T(8,128)(2,1)S(1)}, u32[]{:S(2)}, u32[]{:S(2)}) collective-permute-start(bf16[4,32,128]{2,1,0:T(8,128)(2,1)S(1)} %shard_map.102.refs_0_), channel_id=1, source_target_pairs={{0,12},{1,13},{2,14},{3,15},{4,0},{5,1},{6,2},{7,3},{8,4},{9,5},{1... | collective-permute-start | bytes 98312 | tf_op jit(solution)/shard_map/ppermute | solution.py:394
  139.1 9.1 %all-to-all-done.3.terms = bf16[8,4,32,640]{3,2,1,0:T(8,128)(2,1)S(1)} async-done(((bf16[8,4,32,640]{3,2,1,0:T(8,128)(2,1)}), bf16[8,4,32,640]{3,2,1,0:T(8,128)(2,1)S(1)}, u32[]{:S(2)}, u32[]{:S(2)}) %all-to-all-start.3) | async-done | bytes 1310752 | tf_op jit(solution)/shard_map/all_to_all | solution.py:333
  149.5 3.4 %all-to-all-start.4 = ((bf16[8,4,32,128]{3,2,1,0:T(8,128)(2,1)}), bf16[8,4,32,128]{3,2,1,0:T(8,128)(2,1)S(1)}, u32[]{:S(2)}, u32[]{:S(2)}) async-start(bf16[8,4,32,128]{3,2,1,0:T(8,128)(2,1)} %shard_map.103.mine), calls=%async_computation.4 | async-start | bytes 524288 | tf_op jit(solution)/shard_map/all_to_all | solution.py:333
  154.7 4.4 %all-to-all-done.4.mine = bf16[8,4,32,128]{3,2,1,0:T(8,128)(2,1)S(1)} async-done(((bf16[8,4,32,128]{3,2,1,0:T(8,128)(2,1)}), bf16[8,4,32,128]{3,2,1,0:T(8,128)(2,1)S(1)}, u32[]{:S(2)}, u32[]{:S(2)}) %all-to-all-start.4) | async-done | bytes 262176 | tf_op jit(solution)/shard_map/all_to_all | solution.py:333
  162.9 2.6 %shard_map.105 = bf16[4,64,320]{2,1,0:T(8,128)(2,1)} custom-call(s32[11]{0:T(128)S(1)} %copy-done.5, bf16[8,4,32,128]{3,2,1,0:T(8,128)(2,1)} %shard_map.103.mine, bf16[8,4,32,128]{3,2,1,0:T(8,128)(2,1)S(1)} %collective-permute-done.24.others, f32[4,32,320]{2,1,0:T(8,128)S(1)} %get-tuple-element.59.keep, f32[4,32,320]{2,1,0:T(8,128)S(1)} %collective-permute-done.25.got, ...), custom_call_target="tpu_custom_call" | custom-call | flops 3000000000 | bytes 8388608 | tf_op jit(solution)/shard_map/pallas_call | solution.py:145
  165.5 2.0 %shard_map.106 = f32[4,320,128]{2,1,0:T(8,128)} custom-call(s32[11]{0:T(128)S(1)} %copy-done.5, f32[4]{0:T(128)S(1)} %copy-done.22, bf16[8,4,32,128]{3,2,1,0:T(8,128)(2,1)S(1)} %all-to-all-done.4.mine, bf16[8,4,32,128]{3,2,1,0:T(8,128)(2,1)S(1)} %collective-permute-done.26.others, bf16[8,4,64,384]{3,2,1,0:T(8,128)(2,1)S(1)} %copy-done.1), custom_call_target="tpu_custom_call" | custom-call | flops 3000000000 | bytes 8388608 | tf_op jit(solution)/shard_map/pallas_call | solution.py:145
  167.5 4.1 %add.13 = f32[4,64,3200]{2,1,0:T(8,128)} add(f32[4,64,3200]{2,1,0:T(8,128)S(1)} %copy-done.31, f32[4,64,3200]{2,1,0:T(8,128)} %collective-permute-done.27) | non-fusion elementwise | flops 819200 | bytes 9830400 | tf_op jit(solution)/shard_map/add | solution.py:412
  (121 shorter events, 36.5 us)
Async XLA Ops:
  1.9 11.4 %collective-permute-start = (bf16[2,32,3200]{2,1,0:T(8,128)(2,1)S(1)}, bf16[2,32,3200]{2,1,0:T(8,128)(2,1)S(1)}, u32[]{:S(2)}, u32[]{:S(2)}) collective-permute-start(bf16[2,32,3200]{2,1,0:T(8,128)(2,1)S(1)} %get-tuple-element.64.refs_1_.refs_0_), channel_id=1, source_target_pairs={{0,2},{1,15},{2,4},{3,1},{4,6},{5,3},{6,8},{7,5},{8,10},{9,7},{10,... | collective-permute-start | bytes 1228808 | tf_op jit(solution)/shard_map/ppermute | solution.py:339
  8.4 9.3 %collective-permute-start.3 = (bf16[2,32,3200]{2,1,0:T(8,128)(2,1)S(1)}, bf16[2,32,3200]{2,1,0:T(8,128)(2,1)S(1)}, u32[]{:S(2)}, u32[]{:S(2)}) collective-permute-start(bf16[2,32,3200]{2,1,0:T(8,128)(2,1)S(1)} %get-tuple-element.63.refs_2_.refs_1_), channel_id=1, source_target_pairs={{0,2},{1,15},{2,4},{3,1},{4,6},{5,3},{6,8},{7,5},{8,10},{9,7},{10,... | collective-permute-start | bytes 1228808 | tf_op jit(solution)/shard_map/ppermute | solution.py:339
  17.7 25.7 %collective-permute-start.4 = (bf16[320,3200]{1,0:T(8,128)(2,1)}, bf16[320,3200]{1,0:T(8,128)(2,1)}, u32[]{:S(2)}, u32[]{:S(2)}) collective-permute-start(bf16[320,3200]{1,0:T(8,128)(2,1)} %refs_0_), channel_id=1, source_target_pairs={{0,1},{1,0},{2,3},{3,2},{4,5},{5,4},{6,7},{7,6},{8,9},{9,8},{10,11... | collective-permute-start | bytes 6144008 | tf_op jit(solution)/shard_map/ppermute | solution.py:327
  19.7 23.7 %collective-permute-start.5 = (bf16[256,3200]{1,0:T(8,128)(2,1)}, bf16[256,3200]{1,0:T(8,128)(2,1)}, u32[]{:S(2)}, u32[]{:S(2)}) collective-permute-start(bf16[256,3200]{1,0:T(8,128)(2,1)} %bitcast.3.refs_2_), channel_id=1, source_target_pairs={{0,1},{1,0},{2,3},{3,2},{4,5},{5,4},{6,7},{7,6},{8,9},{9,8},{10,11... | collective-permute-start | bytes 4915208 | tf_op jit(solution)/shard_map/ppermute | solution.py:327
  19.8 7.1 %collective-permute-start.8 = (bf16[2,32,3200]{2,1,0:T(8,128)(2,1)S(1)}, bf16[2,32,3200]{2,1,0:T(8,128)(2,1)S(1)}, u32[]{:S(2)}, u32[]{:S(2)}) collective-permute-start(bf16[2,32,3200]{2,1,0:T(8,128)(2,1)S(1)} %collective-permute-done.3.refs_4_.refs_3_), channel_id=1, source_target_pairs={{0,2},{1,15},{2,4},{3,1},{4,6},{5,3},{6,8},{7,5},{8,10},{9,7},{10,... | collective-permute-start | bytes 1228808 | tf_op jit(solution)/shard_map/ppermute | solution.py:339
  24.5 9.8 %collective-permute-start.16 = (f32[8,4,32,128]{3,2,1,0:T(8,128)S(1)}, f32[8,4,32,128]{3,2,1,0:T(8,128)S(1)}, u32[]{:S(2)}, u32[]{:S(2)}) collective-permute-start(f32[8,4,32,128]{3,2,1,0:T(8,128)S(1)} %get-tuple-element.51), channel_id=1, source_target_pairs={{0,1},{1,0},{2,3},{3,2},{4,5},{5,4},{6,7},{7,6},{8,9},{9,8},{10,11... | collective-permute-start | bytes 1572872 | tf_op jit(solution)/shard_map/ppermute | solution.py:327
  24.6 7.2 %collective-permute-start.1 = (bf16[2,32,3200]{2,1,0:T(8,128)(2,1)S(1)}, bf16[2,32,3200]{2,1,0:T(8,128)(2,1)S(1)}, u32[]{:S(2)}, u32[]{:S(2)}) collective-permute-start(bf16[2,32,3200]{2,1,0:T(8,128)(2,1)S(1)} %collective-permute-done.refs_3_.refs_2_), channel_id=1, source_target_pairs={{0,2},{1,15},{2,4},{3,1},{4,6},{5,3},{6,8},{7,5},{8,10},{9,7},{10,... | collective-permute-start | bytes 1228808 | tf_op jit(solution)/shard_map/ppermute | solution.py:339
  26.9 13.8 %collective-permute-start.9 = (bf16[2,32,3200]{2,1,0:T(8,128)(2,1)S(1)}, bf16[2,32,3200]{2,1,0:T(8,128)(2,1)S(1)}, u32[]{:S(2)}, u32[]{:S(2)}) collective-permute-start(bf16[2,32,3200]{2,1,0:T(8,128)(2,1)S(1)} %collective-permute-done.8.refs_2_.refs_5_), channel_id=1, source_target_pairs={{0,2},{1,15},{2,4},{3,1},{4,6},{5,3},{6,8},{7,5},{8,10},{9,7},{10,... | collective-permute-start | bytes 1228808 | tf_op jit(solution)/shard_map/ppermute | solution.py:339
  31.7 20.6 %collective-permute-start.2 = (bf16[2,32,3200]{2,1,0:T(8,128)(2,1)S(1)}, bf16[2,32,3200]{2,1,0:T(8,128)(2,1)}, u32[]{:S(2)}, u32[]{:S(2)}) collective-permute-start(bf16[2,32,3200]{2,1,0:T(8,128)(2,1)S(1)} %collective-permute-done.1.refs_1_.refs_4_), channel_id=1, source_target_pairs={{0,2},{1,15},{2,4},{3,1},{4,6},{5,3},{6,8},{7,5},{8,10},{9,7},{10,... | collective-permute-start | bytes 1228808 | tf_op jit(solution)/shard_map/ppermute | solution.py:339
  35.1 26.9 %all-to-all-start = ((bf16[8,4,32,128]{3,2,1,0:T(8,128)(2,1)}), bf16[8,4,32,128]{3,2,1,0:T(8,128)(2,1)S(1)}, u32[]{:S(2)}, u32[]{:S(2)}) async-start(bf16[8,4,32,128]{3,2,1,0:T(8,128)(2,1)} %add_convert_fusion), calls=%async_computation | async-start | bytes 524288 | tf_op jit(solution)/shard_map/all_to_all | solution.py:330
  40.7 13.0 %collective-permute-start.11 = (bf16[2,32,3200]{2,1,0:T(8,128)(2,1)S(1)}, bf16[2,32,3200]{2,1,0:T(8,128)(2,1)}, u32[]{:S(2)}, u32[]{:S(2)}) collective-permute-start(bf16[2,32,3200]{2,1,0:T(8,128)(2,1)S(1)} %collective-permute-done.9.refs_4_.refs_7_), channel_id=1, source_target_pairs={{0,2},{1,15},{2,4},{3,1},{4,6},{5,3},{6,8},{7,5},{8,10},{9,7},{10,... | collective-permute-start | bytes 1228808 | tf_op jit(solution)/shard_map/ppermute | solution.py:339
  52.4 7.5 %collective-permute-start.6 = (bf16[2,32,3200]{2,1,0:T(8,128)(2,1)}, bf16[2,32,3200]{2,1,0:T(8,128)(2,1)}, u32[]{:S(2)}, u32[]{:S(2)}) collective-permute-start(bf16[2,32,3200]{2,1,0:T(8,128)(2,1)} %collective-permute-done.2.refs_3_.refs_6_), channel_id=1, source_target_pairs={{0,2},{1,15},{2,4},{3,1},{4,6},{5,3},{6,8},{7,5},{8,10},{9,7},{10,... | collective-permute-start | bytes 1228808 | tf_op jit(solution)/shard_map/ppermute | solution.py:339
  53.7 15.4 %collective-permute-start.12 = (bf16[2,32,3200]{2,1,0:T(8,128)(2,1)}, bf16[2,32,3200]{2,1,0:T(8,128)(2,1)}, u32[]{:S(2)}, u32[]{:S(2)}) collective-permute-start(bf16[2,32,3200]{2,1,0:T(8,128)(2,1)} %collective-permute-done.11.refs_2_.refs_9_), channel_id=1, source_target_pairs={{0,2},{1,15},{2,4},{3,1},{4,6},{5,3},{6,8},{7,5},{8,10},{9,7},{10,... | collective-permute-start | bytes 1228808 | tf_op jit(solution)/shard_map/ppermute | solution.py:339
  59.9 20.4 %collective-permute-start.7 = (bf16[2,32,3200]{2,1,0:T(8,128)(2,1)}, bf16[2,32,3200]{2,1,0:T(8,128)(2,1)}, u32[]{:S(2)}, u32[]{:S(2)}) collective-permute-start(bf16[2,32,3200]{2,1,0:T(8,128)(2,1)} %collective-permute-done.6.refs_1_.refs_8_), channel_id=1, source_target_pairs={{0,2},{1,15},{2,4},{3,1},{4,6},{5,3},{6,8},{7,5},{8,10},{9,7},{10,... | collective-permute-start | bytes 1228808 | tf_op jit(solution)/shard_map/ppermute | solution.py:339
  63.9 39.2 %all-to-all-start.1 = ((bf16[8,4,64,384]{3,2,1,0:T(8,128)(2,1)}), bf16[8,4,64,384]{3,2,1,0:T(8,128)(2,1)S(1)}, u32[]{:S(2)}, u32[]{:S(2)}) async-start(bf16[8,4,64,384]{3,2,1,0:T(8,128)(2,1)} %shard_map.100), calls=%async_computation.1 | async-start | bytes 3145728 | tf_op jit(solution)/shard_map/all_to_all | solution.py:333
  69.1 17.4 %collective-permute-start.13 = (bf16[2,32,3200]{2,1,0:T(8,128)(2,1)}, bf16[2,32,3200]{2,1,0:T(8,128)(2,1)S(1)}, u32[]{:S(2)}, u32[]{:S(2)}) collective-permute-start(bf16[2,32,3200]{2,1,0:T(8,128)(2,1)} %collective-permute-done.12.refs_4_.refs_11_), channel_id=1, source_target_pairs={{0,2},{1,15},{2,4},{3,1},{4,6},{5,3},{6,8},{7,5},{8,10},{9,7},{10,... | collective-permute-start | bytes 1228808 | tf_op jit(solution)/shard_map/ppermute | solution.py:339
  80.2 7.4 %collective-permute-start.10 = (bf16[2,32,3200]{2,1,0:T(8,128)(2,1)}, bf16[2,32,3200]{2,1,0:T(8,128)(2,1)S(1)}, u32[]{:S(2)}, u32[]{:S(2)}) collective-permute-start(bf16[2,32,3200]{2,1,0:T(8,128)(2,1)} %collective-permute-done.7.refs_3_.refs_10_), channel_id=1, source_target_pairs={{0,2},{1,15},{2,4},{3,1},{4,6},{5,3},{6,8},{7,5},{8,10},{9,7},{10,... | collective-permute-start | bytes 1228808 | tf_op jit(solution)/shard_map/ppermute | solution.py:339
  86.5 6.9 %collective-permute-start.15 = (bf16[2,32,3200]{2,1,0:T(8,128)(2,1)S(1)}, bf16[2,32,3200]{2,1,0:T(8,128)(2,1)S(1)}, u32[]{:S(2)}, u32[]{:S(2)}) collective-permute-start(bf16[2,32,3200]{2,1,0:T(8,128)(2,1)S(1)} %collective-permute-done.13.refs_2_.refs_13_), channel_id=1, source_target_pairs={{0,2},{1,15},{2,4},{3,1},{4,6},{5,3},{6,8},{7,5},{8,10},{9,7},{10,... | collective-permute-start | bytes 1228808 | tf_op jit(solution)/shard_map/ppermute | solution.py:339
  87.6 10.5 %collective-permute-start.14 = (bf16[2,32,3200]{2,1,0:T(8,128)(2,1)S(1)}, bf16[2,32,3200]{2,1,0:T(8,128)(2,1)S(1)}, u32[]{:S(2)}, u32[]{:S(2)}) collective-permute-start(bf16[2,32,3200]{2,1,0:T(8,128)(2,1)S(1)} %collective-permute-done.10.refs_1_.refs_12_), channel_id=1, source_target_pairs={{0,2},{1,15},{2,4},{3,1},{4,6},{5,3},{6,8},{7,5},{8,10},{9,7},{10,... | collective-permute-start | bytes 1228808 | tf_op jit(solution)/shard_map/ppermute | solution.py:339
  103.1 14.3 %all-to-all-start.2 = ((bf16[8,4,32,128]{3,2,1,0:T(8,128)(2,1)}), bf16[8,4,32,128]{3,2,1,0:T(8,128)(2,1)S(1)}, u32[]{:S(2)}, u32[]{:S(2)}) async-start(bf16[8,4,32,128]{3,2,1,0:T(8,128)(2,1)} %get-tuple-element.52), calls=%async_computation.2 | async-start | bytes 524288 | tf_op jit(solution)/shard_map/all_to_all | solution.py:333
  118.2 49.4 %collective-permute-start.27 = (f32[4,64,3200]{2,1,0:T(8,128)}, f32[4,64,3200]{2,1,0:T(8,128)}, u32[]{:S(2)}, u32[]{:S(2)}) collective-permute-start(f32[4,64,3200]{2,1,0:T(8,128)} %get-tuple-element.62), channel_id=1, source_target_pairs={{0,1},{1,0},{2,3},{3,2},{4,5},{5,4},{6,7},{7,6},{8,9},{9,8},{10,11... | collective-permute-start | bytes 9830408 | tf_op jit(solution)/shard_map/ppermute | solution.py:327
  124.1 24.1 %all-to-all-start.3 = ((bf16[8,4,32,640]{3,2,1,0:T(8,128)(2,1)}), bf16[8,4,32,640]{3,2,1,0:T(8,128)(2,1)S(1)}, u32[]{:S(2)}, u32[]{:S(2)}) async-start(bf16[8,4,32,640]{3,2,1,0:T(8,128)(2,1)} %get-tuple-element.57), calls=%async_computation.3 | async-start | bytes 2621440 | tf_op jit(solution)/shard_map/all_to_all | solution.py:333
  129.5 7.1 %collective-permute-start.17 = (bf16[4,32,128]{2,1,0:T(8,128)(2,1)S(1)}, bf16[4,32,128]{2,1,0:T(8,128)(2,1)S(1)}, u32[]{:S(2)}, u32[]{:S(2)}) collective-permute-start(bf16[4,32,128]{2,1,0:T(8,128)(2,1)S(1)} %shard_map.102.refs_0_), channel_id=1, source_target_pairs={{0,2},{1,3},{2,4},{3,5},{4,6},{5,7},{6,8},{7,9},{8,10},{9,11},{10,... | collective-permute-start | bytes 98312 | tf_op jit(solution)/shard_map/ppermute | solution.py:394
  130.9 5.8 %collective-permute-start.18 = (bf16[4,32,128]{2,1,0:T(8,128)(2,1)S(1)}, bf16[4,32,128]{2,1,0:T(8,128)(2,1)S(1)}, u32[]{:S(2)}, u32[]{:S(2)}) collective-permute-start(bf16[4,32,128]{2,1,0:T(8,128)(2,1)S(1)} %shard_map.102.refs_0_), channel_id=1, source_target_pairs={{0,4},{1,5},{2,6},{3,7},{4,8},{5,9},{6,10},{7,11},{8,12},{9,13},{1... | collective-permute-start | bytes 98312 | tf_op jit(solution)/shard_map/ppermute | solution.py:394
  130.9 17.2 %collective-permute-start.19 = (bf16[4,32,128]{2,1,0:T(8,128)(2,1)S(1)}, bf16[4,32,128]{2,1,0:T(8,128)(2,1)S(1)}, u32[]{:S(2)}, u32[]{:S(2)}) collective-permute-start(bf16[4,32,128]{2,1,0:T(8,128)(2,1)S(1)} %shard_map.102.refs_0_), channel_id=1, source_target_pairs={{0,6},{1,7},{2,8},{3,9},{4,10},{5,11},{6,12},{7,13},{8,14},{9,15},... | collective-permute-start | bytes 98312 | tf_op jit(solution)/shard_map/ppermute | solution.py:394
  132.4 15.8 %collective-permute-start.20 = (bf16[4,32,128]{2,1,0:T(8,128)(2,1)S(1)}, bf16[4,32,128]{2,1,0:T(8,128)(2,1)S(1)}, u32[]{:S(2)}, u32[]{:S(2)}) collective-permute-start(bf16[4,32,128]{2,1,0:T(8,128)(2,1)S(1)} %shard_map.102.refs_0_), channel_id=1, source_target_pairs={{0,8},{1,9},{2,10},{3,11},{4,12},{5,13},{6,14},{7,15},{8,0},{9,1},... | collective-permute-start | bytes 98312 | tf_op jit(solution)/shard_map/ppermute | solution.py:394
  136.6 11.6 %collective-permute-start.21 = (bf16[4,32,128]{2,1,0:T(8,128)(2,1)S(1)}, bf16[4,32,128]{2,1,0:T(8,128)(2,1)S(1)}, u32[]{:S(2)}, u32[]{:S(2)}) collective-permute-start(bf16[4,32,128]{2,1,0:T(8,128)(2,1)S(1)} %shard_map.102.refs_0_), channel_id=1, source_target_pairs={{0,10},{1,11},{2,12},{3,13},{4,14},{5,15},{6,0},{7,1},{8,2},{9,3},... | collective-permute-start | bytes 98312 | tf_op jit(solution)/shard_map/ppermute | solution.py:394
  136.7 11.5 %collective-permute-start.22 = (bf16[4,32,128]{2,1,0:T(8,128)(2,1)S(1)}, bf16[4,32,128]{2,1,0:T(8,128)(2,1)S(1)}, u32[]{:S(2)}, u32[]{:S(2)}) collective-permute-start(bf16[4,32,128]{2,1,0:T(8,128)(2,1)S(1)} %shard_map.102.refs_0_), channel_id=1, source_target_pairs={{0,12},{1,13},{2,14},{3,15},{4,0},{5,1},{6,2},{7,3},{8,4},{9,5},{1... | collective-permute-start | bytes 98312 | tf_op jit(solution)/shard_map/ppermute | solution.py:394
  149.5 9.7 %all-to-all-start.4 = ((bf16[8,4,32,128]{3,2,1,0:T(8,128)(2,1)}), bf16[8,4,32,128]{3,2,1,0:T(8,128)(2,1)S(1)}, u32[]{:S(2)}, u32[]{:S(2)}) async-start(bf16[8,4,32,128]{3,2,1,0:T(8,128)(2,1)} %shard_map.103.mine), calls=%async_computation.4 | async-start | bytes 524288 | tf_op jit(solution)/shard_map/all_to_all | solution.py:333
  152.9 8.2 %collective-permute-start.24 = (bf16[8,4,32,128]{3,2,1,0:T(8,128)(2,1)}, bf16[8,4,32,128]{3,2,1,0:T(8,128)(2,1)S(1)}, u32[]{:S(2)}, u32[]{:S(2)}) collective-permute-start(bf16[8,4,32,128]{3,2,1,0:T(8,128)(2,1)} %shard_map.103.mine), channel_id=1, source_target_pairs={{0,1},{1,0},{2,3},{3,2},{4,5},{5,4},{6,7},{7,6},{8,9},{9,8},{10,11... | collective-permute-start | bytes 786440 | tf_op jit(solution)/shard_map/ppermute | solution.py:327
  154.6 6.5 %collective-permute-start.25 = (f32[4,32,320]{2,1,0:T(8,128)S(1)}, f32[4,32,320]{2,1,0:T(8,128)S(1)}, u32[]{:S(2)}, u32[]{:S(2)}) collective-permute-start(f32[4,32,320]{2,1,0:T(8,128)S(1)} %get-tuple-element.60), channel_id=1, source_target_pairs={{0,1},{1,0},{2,3},{3,2},{4,5},{5,4},{6,7},{7,6},{8,9},{9,8},{10,11... | collective-permute-start | bytes 491528 | tf_op jit(solution)/shard_map/ppermute | solution.py:327
  159.2 6.3 %collective-permute-start.26 = (bf16[8,4,32,128]{3,2,1,0:T(8,128)(2,1)S(1)}, bf16[8,4,32,128]{3,2,1,0:T(8,128)(2,1)S(1)}, u32[]{:S(2)}, u32[]{:S(2)}) collective-permute-start(bf16[8,4,32,128]{3,2,1,0:T(8,128)(2,1)S(1)} %all-to-all-done.4.mine), channel_id=1, source_target_pairs={{0,1},{1,0},{2,3},{3,2},{4,5},{5,4},{6,7},{7,6},{8,9},{9,8},{10,11... | collective-permute-start | bytes 786440 | tf_op jit(solution)/shard_map/ppermute | solution.py:327
  (35 other events, 437.8 us)

commit v2 on v1

--- a/solution.py
+++ b/solution.py
@@ -357,13 +357,12 @@
     keep, give = small_call(
         hidden_kernel,
         (shape(piece, F32), shape(piece, F32)),
-        (place, after(x, own[1][0]), lefts),
-    )
-    terms = over_planes((keep + swap(give)).astype(BF16))
+        (place, after(x, *own[0]), lefts),
+    )
+    mixed = (keep + swap(give)).astype(BF16)
+    terms = over_planes(mixed)
     own.append(passed_on(own[2]))
-    weights = kept_in_vmem(weights)
-    products = step_products((0, 1), place, own[0] + own[1], weights, ())
-    own[3][0] = after(own[3][0], *products)
+    own[3][1] = after(own[3][1], terms)
     own.append(passed_on(own[3]))
     wide = (slots, tokens, feats + ranks)
     shared = small_call(
@@ -372,9 +371,11 @@
         (place, terms, x),
         scratch=(pltpu.VMEM(wide, BF16), sems),
     )
+    own[4][1] = after(own[4][1], shared)
     shared = over_rows(shared)
     own.append(passed_on(own[4]))
-    products = step_products((2, 3), place, own[2] + own[3], weights, products)
+    weights = kept_in_vmem(weights)
+    products = step_products((0, 1, 2, 3), place, sum(own[:4], []), weights, ())
     own[5][0] = after(own[5][0], *products)
     own.append(passed_on(own[5]))
     products = step_products((4, 5), place, own[4] + own[5], weights, products)
@@ -410,6 +411,7 @@
         (place, factor_planes, swap(factor_planes), keep, swap(give), lefts),
     )
     grad_b = keep_b + got_b
+    factor_tokens = after(factor_tokens, grad_in, grad_b)
     grad_a = small_call(
         grad_a_kernel,
         shape((slots, feats, 2 * ranks), F32),

time: 173 us -> 159 us (0.919)
  local copies, waits for them, and re-layouts: 13.2 us -> 5.68 us
  starting transfers between devices: 72.7 us -> 67.1 us
    unnamed x68 -> x52, local copies, waits for them, and re-layouts: 11.9 us -> 4.38 us
    ppermute x14, waiting for transfers between devices: 24.7 us -> 32 us  [passed_on(): return [lax.ppermute(unit, 'col', RING) for unit in units]]
    all_to_all x4, waiting for transfers between devices: 13.5 us -> 6.57 us  [over_rows(): return lax.all_to_all(pieces, 'row', 0, 0)]
    ppermute x14, starting transfers between devices: 27.5 us -> 24.1 us  [passed_on(): return [lax.ppermute(unit, 'col', RING) for unit in units]]
    ppermute x7, starting transfers between devices: 10.9 us -> 7.6 us  [swap(): return lax.ppermute(piece, 'col', SWAP)]
    ppermute x7, starting transfers between devices: 9.64 us -> 12.1 us  [body(): lax.ppermute(factor, 'col', [(c, (c + 2 * hop) % 16) for c in range(16)])]
    pallas_call x4 -> x3, Pallas kernels: 18.2 us -> 16.6 us  [step_products(): pl.pallas_call(kernel, out_shape=(jax.ShapeDtypeStruct((ROWS,) + main_sha...]
  transfers between devices with their start and end apart: 33 -> 33, of which waited for: 10 -> 11; matrix products, arithmetic and copies ran while one was open for 1% -> 4% of each run, Pallas kernels for 23% -> 23%
where the time goes in v2:
time: 159 us
  starting transfers between devices  67.1 us (42%)
  waiting for transfers between devices  39.8 us (25%)
  Pallas kernels  39.6 us (25%)
  local copies, waits for them, and re-layouts  5.68 us (4%)
  other arithmetic  5.56 us (3%)
    ppermute x14, waiting for transfers between devices, passed_on(): return [lax.ppermute(unit, 'col', RING) for unit in units]  32 us
    ppermute x14, starting transfers between devices, passed_on(): return [lax.ppermute(unit, 'col', RING) for unit in units]  24.1 us
    all_to_all x4, starting transfers between devices, over_rows(): return lax.all_to_all(pieces, 'row', 0, 0)  18.9 us
    pallas_call x3, Pallas kernels, step_products(): pl.pallas_call(kernel, out_shape=(jax.ShapeDtypeStruct((ROWS,) + main_sha...  16.6 us
    ppermute x7, starting transfers between devices, body(): lax.ppermute(factor, 'col', [(c, (c + 2 * hop) % 16) for c in range(16)])  12.1 us
    pallas_call x7, Pallas kernels, small_call(): pl.pallas_call(kernel, out_shape=out_shape, in_specs=[SMEM] * scalars + [...  10.5 us
    pallas_call x1, Pallas kernels, grad_b_parts(): pl.pallas_call(grad_b_kernel, out_shape=(part, part), in_specs=[SMEM, SME...  9.25 us
    ppermute x7, starting transfers between devices, swap(): return lax.ppermute(piece, 'col', SWAP)  7.6 us
  transfers between devices with their start and end apart: 33, of which 11 were waited for; matrix products, arithmetic and copies ran while one was open for 4% of the time, Pallas kernels for 23%

profile of v2, /device:TPU:1, one launch (start us, length us, event | category | flops | bytes accessed | tf_op | source)
XLA Modules:
  0.0 158.8 jit_solution(90069803342789632)
XLA Ops:
  1.9 6.5 %collective-permute-start.5 = (bf16[2,32,3200]{2,1,0:T(8,128)(2,1)S(1)}, bf16[2,32,3200]{2,1,0:T(8,128)(2,1)S(1)}, u32[]{:S(2)}, u32[]{:S(2)}) collective-permute-start(bf16[2,32,3200]{2,1,0:T(8,128)(2,1)S(1)} %get-tuple-element.63.refs_2_.refs_1_), channel_id=1, source_target_pairs={{0,2},{1,15},{2,4},{3,1},{4,6},{5,3},{6,8},{7,5},{8,10},{9,7},{10,... | collective-permute-start | bytes 1228808 | tf_op jit(solution)/shard_map/ppermute | solution.py:339
  9.2 1.7 %copy-done.6 = bf16[4,320,1024]{2,1,0:T(8,128)(2,1)S(1)} copy-done((bf16[4,320,1024]{2,1,0:T(8,128)(2,1)S(1)}, bf16[4,320,1024]{2,1,0:T(8,128)(2,1)}, u32[]{:S(2)}) %copy-start.6) | copy-done | bytes 2621464
  13.3 4.4 %collective-permute-done.refs_3_.refs_2_ = bf16[2,32,3200]{2,1,0:T(8,128)(2,1)S(1)} collective-permute-done((bf16[2,32,3200]{2,1,0:T(8,128)(2,1)S(1)}, bf16[2,32,3200]{2,1,0:T(8,128)(2,1)S(1)}, u32[]{:S(2)}, u32[]{:S(2)}) %collective-permute-start) | collective-permute-done | bytes 409632 | tf_op jit(solution)/shard_map/ppermute | solution.py:339
  17.7 2.0 %collective-permute-start.9 = (bf16[320,3200]{1,0:T(8,128)(2,1)}, bf16[320,3200]{1,0:T(8,128)(2,1)}, u32[]{:S(2)}, u32[]{:S(2)}) collective-permute-start(bf16[320,3200]{1,0:T(8,128)(2,1)} %refs_0_), channel_id=1, source_target_pairs={{0,1},{1,0},{2,3},{3,2},{4,5},{5,4},{6,7},{7,6},{8,9},{9,8},{10,11... | collective-permute-start | bytes 6144008 | tf_op jit(solution)/shard_map/ppermute | solution.py:327
  22.2 4.4 %all-to-all-start = ((bf16[8,4,32,128]{3,2,1,0:T(8,128)(2,1)}), bf16[8,4,32,128]{3,2,1,0:T(8,128)(2,1)S(1)}, u32[]{:S(2)}, u32[]{:S(2)}) async-start(bf16[8,4,32,128]{3,2,1,0:T(8,128)(2,1)} %add_convert_fusion), calls=%async_computation | async-start | bytes 524288 | tf_op jit(solution)/shard_map/all_to_all | solution.py:330
  26.6 2.7 %collective-permute-start.1 = (bf16[2,32,3200]{2,1,0:T(8,128)(2,1)S(1)}, bf16[2,32,3200]{2,1,0:T(8,128)(2,1)S(1)}, u32[]{:S(2)}, u32[]{:S(2)}) collective-permute-start(bf16[2,32,3200]{2,1,0:T(8,128)(2,1)S(1)} %collective-permute-done.refs_3_.refs_2_), channel_id=1, source_target_pairs={{0,2},{1,15},{2,4},{3,1},{4,6},{5,3},{6,8},{7,5},{8,10},{9,7},{10,... | collective-permute-start | bytes 1228808 | tf_op jit(solution)/shard_map/ppermute | solution.py:339
  30.5 9.1 %collective-permute-done.1.refs_5_.refs_4_ = bf16[2,32,3200]{2,1,0:T(8,128)(2,1)S(1)} collective-permute-done((bf16[2,32,3200]{2,1,0:T(8,128)(2,1)S(1)}, bf16[2,32,3200]{2,1,0:T(8,128)(2,1)S(1)}, u32[]{:S(2)}, u32[]{:S(2)}) %collective-permute-start.1) | collective-permute-done | bytes 409632 | tf_op jit(solution)/shard_map/ppermute | solution.py:339
  40.4 3.5 %collective-permute-done.7.refs_8_.refs_7_ = bf16[2,32,3200]{2,1,0:T(8,128)(2,1)S(1)} collective-permute-done((bf16[2,32,3200]{2,1,0:T(8,128)(2,1)S(1)}, bf16[2,32,3200]{2,1,0:T(8,128)(2,1)S(1)}, u32[]{:S(2)}, u32[]{:S(2)}) %collective-permute-start.7) | collective-permute-done | bytes 409632 | tf_op jit(solution)/shard_map/ppermute | solution.py:339
  44.8 1.9 %shard_map.97 = bf16[8,4,64,384]{3,2,1,0:T(8,128)(2,1)} custom-call(s32[11]{0:T(128)S(1)} %concatenate.3.place.refs_0_, bf16[8,4,32,128]{3,2,1,0:T(8,128)(2,1)S(1)} %all-to-all-done.terms, bf16[4,64,320]{2,1,0:T(8,128)(2,1)S(1)} %copy-done.21), custom_call_target="tpu_custom_call" | custom-call | flops 3000000000 | bytes 8388608 | tf_op jit(solution)/shard_map/pallas_call | solution.py:145
  49.3 3.5 %collective-permute-done.12.refs_2_.refs_9_ = bf16[2,32,3200]{2,1,0:T(8,128)(2,1)} collective-permute-done((bf16[2,32,3200]{2,1,0:T(8,128)(2,1)S(1)}, bf16[2,32,3200]{2,1,0:T(8,128)(2,1)}, u32[]{:S(2)}, u32[]{:S(2)}) %collective-permute-start.12) | collective-permute-done | bytes 409632 | tf_op jit(solution)/shard_map/ppermute | solution.py:339
  53.7 5.0 %all-to-all-start.1 = ((bf16[8,4,64,384]{3,2,1,0:T(8,128)(2,1)}), bf16[8,4,64,384]{3,2,1,0:T(8,128)(2,1)S(1)}, u32[]{:S(2)}, u32[]{:S(2)}) async-start(bf16[8,4,64,384]{3,2,1,0:T(8,128)(2,1)} %shard_map.97), calls=%async_computation.1 | async-start | bytes 3145728 | tf_op jit(solution)/shard_map/all_to_all | solution.py:333
  58.8 1.8 %collective-permute-start.4 = (bf16[2,32,3200]{2,1,0:T(8,128)(2,1)}, bf16[2,32,3200]{2,1,0:T(8,128)(2,1)S(1)}, u32[]{:S(2)}, u32[]{:S(2)}) collective-permute-start(bf16[2,32,3200]{2,1,0:T(8,128)(2,1)} %collective-permute-done.3.refs_1_.refs_8_), channel_id=1, source_target_pairs={{0,2},{1,15},{2,4},{3,1},{4,6},{5,3},{6,8},{7,5},{8,10},{9,7},{10,... | collective-permute-start | bytes 1228808 | tf_op jit(solution)/shard_map/ppermute | solution.py:339
  62.5 3.2 %shard_map.95 = (bf16[320,3200]{1,0:T(8,128)(2,1)S(1)}, bf16[320,3200]{1,0:T(8,128)(2,1)S(1)}, bf16[256,3200]{1,0:T(8,128)(2,1)S(1)}, bf16[256,3200]{1,0:T(8,128)(2,1)S(1)}) custom-call(bf16[320,3200]{1,0:T(8,128)(2,1)} %refs_0_, bf16[320,3200]{1,0:T(8,128)(2,1)} %collective-permute-done.9.refs_1_, bf16[256,3200]{1,0:T(8,128)(2,1)} %bitcast.3.refs_2_, ...), custom_call_target="tpu_custom_call" | custom-call | flops 3000000000 | bytes 8388608 | tf_op jit(solution)/shard_map/pallas_call | solution.py:53
  65.8 7.4 %shard_map.96 = (bf16[8,4,32,640]{3,2,1,0:T(8,128)(2,1)}, bf16[8,4,32,128]{3,2,1,0:T(8,128)(2,1)}) custom-call(s32[11]{0:T(128)S(1)} %concatenate.3.place.refs_0_, bf16[2,32,3200]{2,1,0:T(8,128)(2,1)S(1)} %get-tuple-element.64.refs_1_.refs_0_, bf16[2,32,3200]{2,1,0:T(8,128)(2,1)S(1)} %get-tuple-element.63.refs_2_.refs_1_, ...), custom_call_target="tpu_custom_call" | custom-call | flops 3000000000 | bytes 8388608 | tf_op jit(solution)/shard_map/pallas_call | solution.py:122
  73.2 1.8 %collective-permute-start.11 = (bf16[2,32,3200]{2,1,0:T(8,128)(2,1)S(1)}, bf16[2,32,3200]{2,1,0:T(8,128)(2,1)S(1)}, u32[]{:S(2)}, u32[]{:S(2)}) collective-permute-start(bf16[2,32,3200]{2,1,0:T(8,128)(2,1)S(1)} %collective-permute-done.4.refs_3_.refs_10_), channel_id=1, source_target_pairs={{0,2},{1,15},{2,4},{3,1},{4,6},{5,3},{6,8},{7,5},{8,10},{9,7},{10,... | collective-permute-start | bytes 1228808 | tf_op jit(solution)/shard_map/ppermute | solution.py:339
  75.0 4.9 %shard_map.98 = (bf16[8,4,32,640]{3,2,1,0:T(8,128)(2,1)}, bf16[8,4,32,128]{3,2,1,0:T(8,128)(2,1)}) custom-call(s32[11]{0:T(128)S(1)} %concatenate.3.place.refs_0_, bf16[2,32,3200]{2,1,0:T(8,128)(2,1)} %collective-permute-done.3.refs_1_.refs_8_, ...), custom_call_target="tpu_custom_call", output_to_operand_aliasing={{0}: (9, {}), {1}: (10, {})} | custom-call | flops 3000000000 | bytes 8388608 | tf_op jit(solution)/shard_map/pallas_call | solution.py:122
  81.3 1.8 %collective-permute-start.15 = (bf16[2,32,3200]{2,1,0:T(8,128)(2,1)S(1)}, bf16[2,32,3200]{2,1,0:T(8,128)(2,1)S(1)}, u32[]{:S(2)}, u32[]{:S(2)}) collective-permute-start(bf16[2,32,3200]{2,1,0:T(8,128)(2,1)S(1)} %collective-permute-done.11.refs_1_.refs_12_), channel_id=1, source_target_pairs={{0,2},{1,15},{2,4},{3,1},{4,6},{5,3},{6,8},{7,5},{8,10},{9,7},{10,... | collective-permute-start | bytes 1228808 | tf_op jit(solution)/shard_map/ppermute | solution.py:339
  83.6 3.6 %collective-permute-done.16.refs_4_.refs_15_ = bf16[2,32,3200]{2,1,0:T(8,128)(2,1)S(1)} collective-permute-done((bf16[2,32,3200]{2,1,0:T(8,128)(2,1)S(1)}, bf16[2,32,3200]{2,1,0:T(8,128)(2,1)S(1)}, u32[]{:S(2)}, u32[]{:S(2)}) %collective-permute-start.16) | collective-permute-done | bytes 409632 | tf_op jit(solution)/shard_map/ppermute | solution.py:339
  87.2 4.4 %collective-permute-done.15.refs_3_.refs_14_ = bf16[2,32,3200]{2,1,0:T(8,128)(2,1)S(1)} collective-permute-done((bf16[2,32,3200]{2,1,0:T(8,128)(2,1)S(1)}, bf16[2,32,3200]{2,1,0:T(8,128)(2,1)S(1)}, u32[]{:S(2)}, u32[]{:S(2)}) %collective-permute-start.15) | collective-permute-done | bytes 409632 | tf_op jit(solution)/shard_map/ppermute | solution.py:339
  91.6 4.2 %shard_map.99 = (bf16[8,4,32,640]{3,2,1,0:T(8,128)(2,1)}, bf16[8,4,32,128]{3,2,1,0:T(8,128)(2,1)}) custom-call(s32[11]{0:T(128)S(1)} %concatenate.3.place.refs_0_, bf16[2,32,3200]{2,1,0:T(8,128)(2,1)S(1)} %collective-permute-done.11.refs_1_.refs_12_, ...), custom_call_target="tpu_custom_call", output_to_operand_aliasing={{0}: (9, {}), {1}: (10, {})} | custom-call | flops 3000000000 | bytes 8388608 | tf_op jit(solution)/shard_map/pallas_call | solution.py:122
  96.7 5.0 %all-to-all-start.2 = ((bf16[8,4,32,128]{3,2,1,0:T(8,128)(2,1)}), bf16[8,4,32,128]{3,2,1,0:T(8,128)(2,1)S(1)}, u32[]{:S(2)}, u32[]{:S(2)}) async-start(bf16[8,4,32,128]{3,2,1,0:T(8,128)(2,1)} %get-tuple-element.51), calls=%async_computation.2 | async-start | bytes 524288 | tf_op jit(solution)/shard_map/all_to_all | solution.py:333
  101.7 9.3 %shard_map.100 = (f32[4,64,3200]{2,1,0:T(8,128)}, f32[4,64,3200]{2,1,0:T(8,128)}) custom-call(s32[11]{0:T(128)} %copy-done.4, f32[4]{0:T(128)} %convert_rsqrt_fusion.scales, bf16[8,4,64,384]{3,2,1,0:T(8,128)(2,1)} %copy-done, bf16[2,32,3200]{2,1,0:T(8,128)(2,1)} %copy-done.3, bf16[2,32,3200]{2,1,0:T(8,128)(2,1)} %copy-done.2, ...), custom_call_target="tpu_custom_call" | custom-call | flops 3000000000 | bytes 8388608 | tf_op jit(solution)/shard_map/pallas_call | solution.py:304
  111.7 4.0 %collective-permute-start.26 = (f32[4,64,3200]{2,1,0:T(8,128)}, f32[4,64,3200]{2,1,0:T(8,128)}, u32[]{:S(2)}, u32[]{:S(2)}) collective-permute-start(f32[4,64,3200]{2,1,0:T(8,128)} %get-tuple-element.61), channel_id=1, source_target_pairs={{0,1},{1,0},{2,3},{3,2},{4,5},{5,4},{6,7},{7,6},{8,9},{9,8},{10,11... | collective-permute-start | bytes 9830408 | tf_op jit(solution)/shard_map/ppermute | solution.py:327
  115.6 5.4 %all-to-all-start.3 = ((bf16[8,4,32,640]{3,2,1,0:T(8,128)(2,1)}), bf16[8,4,32,640]{3,2,1,0:T(8,128)(2,1)S(1)}, u32[]{:S(2)}, u32[]{:S(2)}) async-start(bf16[8,4,32,640]{3,2,1,0:T(8,128)(2,1)} %get-tuple-element.56), calls=%async_computation.3 | async-start | bytes 2621440 | tf_op jit(solution)/shard_map/all_to_all | solution.py:333
  125.4 3.0 %collective-permute-start.20 = (bf16[4,32,128]{2,1,0:T(8,128)(2,1)S(1)}, bf16[4,32,128]{2,1,0:T(8,128)(2,1)S(1)}, u32[]{:S(2)}, u32[]{:S(2)}) collective-permute-start(bf16[4,32,128]{2,1,0:T(8,128)(2,1)S(1)} %shard_map.101.refs_0_), channel_id=1, source_target_pairs={{0,8},{1,9},{2,10},{3,11},{4,12},{5,13},{6,14},{7,15},{8,0},{9,1},... | collective-permute-start | bytes 98312 | tf_op jit(solution)/shard_map/ppermute | solution.py:395
  128.4 2.5 %collective-permute-start.21 = (bf16[4,32,128]{2,1,0:T(8,128)(2,1)S(1)}, bf16[4,32,128]{2,1,0:T(8,128)(2,1)S(1)}, u32[]{:S(2)}, u32[]{:S(2)}) collective-permute-start(bf16[4,32,128]{2,1,0:T(8,128)(2,1)S(1)} %shard_map.101.refs_0_), channel_id=1, source_target_pairs={{0,10},{1,11},{2,12},{3,13},{4,14},{5,15},{6,0},{7,1},{8,2},{9,3},... | collective-permute-start | bytes 98312 | tf_op jit(solution)/shard_map/ppermute | solution.py:395
  131.0 2.2 %collective-permute-start.22 = (bf16[4,32,128]{2,1,0:T(8,128)(2,1)S(1)}, bf16[4,32,128]{2,1,0:T(8,128)(2,1)S(1)}, u32[]{:S(2)}, u32[]{:S(2)}) collective-permute-start(bf16[4,32,128]{2,1,0:T(8,128)(2,1)S(1)} %shard_map.101.refs_0_), channel_id=1, source_target_pairs={{0,12},{1,13},{2,14},{3,15},{4,0},{5,1},{6,2},{7,3},{8,4},{9,5},{1... | collective-permute-start | bytes 98312 | tf_op jit(solution)/shard_map/ppermute | solution.py:395
  133.2 6.6 %all-to-all-done.3.terms = bf16[8,4,32,640]{3,2,1,0:T(8,128)(2,1)S(1)} async-done(((bf16[8,4,32,640]{3,2,1,0:T(8,128)(2,1)}), bf16[8,4,32,640]{3,2,1,0:T(8,128)(2,1)S(1)}, u32[]{:S(2)}, u32[]{:S(2)}) %all-to-all-start.3) | async-done | bytes 1310752 | tf_op jit(solution)/shard_map/all_to_all | solution.py:333
  142.8 3.4 %all-to-all-start.4 = ((bf16[8,4,32,128]{3,2,1,0:T(8,128)(2,1)}), bf16[8,4,32,128]{3,2,1,0:T(8,128)(2,1)S(1)}, u32[]{:S(2)}, u32[]{:S(2)}) async-start(bf16[8,4,32,128]{3,2,1,0:T(8,128)(2,1)} %shard_map.102.mine), calls=%async_computation.4 | async-start | bytes 524288 | tf_op jit(solution)/shard_map/all_to_all | solution.py:333
  148.0 2.7 %shard_map.104 = bf16[4,64,320]{2,1,0:T(8,128)(2,1)} custom-call(s32[11]{0:T(128)S(1)} %copy-done.5, bf16[8,4,32,128]{3,2,1,0:T(8,128)(2,1)} %shard_map.102.mine, bf16[8,4,32,128]{3,2,1,0:T(8,128)(2,1)S(1)} %collective-permute-done.24.others, f32[4,32,320]{2,1,0:T(8,128)S(1)} %get-tuple-element.58.keep, f32[4,32,320]{2,1,0:T(8,128)S(1)} %collective-permute-done.25.got, ...), custom_call_target="tpu_custom_call" | custom-call | flops 3000000000 | bytes 8388608 | tf_op jit(solution)/shard_map/pallas_call | solution.py:145
  150.7 4.3 %add.13 = f32[4,64,3200]{2,1,0:T(8,128)} add(f32[4,64,3200]{2,1,0:T(8,128)S(1)} %copy-done.23, f32[4,64,3200]{2,1,0:T(8,128)} %collective-permute-done.26) | non-fusion elementwise | flops 819200 | bytes 9830400 | tf_op jit(solution)/shard_map/add | solution.py:413
  156.8 2.0 %shard_map.105 = f32[4,320,128]{2,1,0:T(8,128)} custom-call(s32[11]{0:T(128)S(1)} %copy-done.5, f32[4]{0:T(128)S(1)} %copy-done.22, bf16[8,4,32,128]{3,2,1,0:T(8,128)(2,1)S(1)} %all-to-all-done.4.mine, bf16[8,4,32,128]{3,2,1,0:T(8,128)(2,1)S(1)} %collective-permute-done.27.others, bf16[8,4,64,384]{3,2,1,0:T(8,128)(2,1)S(1)} %copy-done.1), custom_call_target="tpu_custom_call" | custom-call | flops 3000000000 | bytes 8388608 | tf_op jit(solution)/shard_map/pallas_call | solution.py:145
  (104 shorter events, 29.5 us)
Async XLA Ops:
  1.9 11.4 %collective-permute-start.5 = (bf16[2,32,3200]{2,1,0:T(8,128)(2,1)S(1)}, bf16[2,32,3200]{2,1,0:T(8,128)(2,1)S(1)}, u32[]{:S(2)}, u32[]{:S(2)}) collective-permute-start(bf16[2,32,3200]{2,1,0:T(8,128)(2,1)S(1)} %get-tuple-element.63.refs_2_.refs_1_), channel_id=1, source_target_pairs={{0,2},{1,15},{2,4},{3,1},{4,6},{5,3},{6,8},{7,5},{8,10},{9,7},{10,... | collective-permute-start | bytes 1228808 | tf_op jit(solution)/shard_map/ppermute | solution.py:339
  8.4 9.3 %collective-permute-start = (bf16[2,32,3200]{2,1,0:T(8,128)(2,1)S(1)}, bf16[2,32,3200]{2,1,0:T(8,128)(2,1)S(1)}, u32[]{:S(2)}, u32[]{:S(2)}) collective-permute-start(bf16[2,32,3200]{2,1,0:T(8,128)(2,1)S(1)} %get-tuple-element.64.refs_1_.refs_0_), channel_id=1, source_target_pairs={{0,2},{1,15},{2,4},{3,1},{4,6},{5,3},{6,8},{7,5},{8,10},{9,7},{10,... | collective-permute-start | bytes 1228808 | tf_op jit(solution)/shard_map/ppermute | solution.py:339
  12.2 9.3 %collective-permute-start.8 = (f32[8,4,32,128]{3,2,1,0:T(8,128)S(1)}, f32[8,4,32,128]{3,2,1,0:T(8,128)S(1)}, u32[]{:S(2)}, u32[]{:S(2)}) collective-permute-start(f32[8,4,32,128]{3,2,1,0:T(8,128)S(1)} %get-tuple-element.35), channel_id=1, source_target_pairs={{0,1},{1,0},{2,3},{3,2},{4,5},{5,4},{6,7},{7,6},{8,9},{9,8},{10,11... | collective-permute-start | bytes 1572872 | tf_op jit(solution)/shard_map/ppermute | solution.py:327
  17.7 44.8 %collective-permute-start.9 = (bf16[320,3200]{1,0:T(8,128)(2,1)}, bf16[320,3200]{1,0:T(8,128)(2,1)}, u32[]{:S(2)}, u32[]{:S(2)}) collective-permute-start(bf16[320,3200]{1,0:T(8,128)(2,1)} %refs_0_), channel_id=1, source_target_pairs={{0,1},{1,0},{2,3},{3,2},{4,5},{5,4},{6,7},{7,6},{8,9},{9,8},{10,11... | collective-permute-start | bytes 6144008 | tf_op jit(solution)/shard_map/ppermute | solution.py:327
  19.7 9.6 %collective-permute-start.6 = (bf16[2,32,3200]{2,1,0:T(8,128)(2,1)S(1)}, bf16[2,32,3200]{2,1,0:T(8,128)(2,1)S(1)}, u32[]{:S(2)}, u32[]{:S(2)}) collective-permute-start(bf16[2,32,3200]{2,1,0:T(8,128)(2,1)S(1)} %collective-permute-done.5.refs_4_.refs_3_), channel_id=1, source_target_pairs={{0,2},{1,15},{2,4},{3,1},{4,6},{5,3},{6,8},{7,5},{8,10},{9,7},{10,... | collective-permute-start | bytes 1228808 | tf_op jit(solution)/shard_map/ppermute | solution.py:339
  21.4 41.1 %collective-permute-start.10 = (bf16[256,3200]{1,0:T(8,128)(2,1)}, bf16[256,3200]{1,0:T(8,128)(2,1)}, u32[]{:S(2)}, u32[]{:S(2)}) collective-permute-start(bf16[256,3200]{1,0:T(8,128)(2,1)} %bitcast.3.refs_2_), channel_id=1, source_target_pairs={{0,1},{1,0},{2,3},{3,2},{4,5},{5,4},{6,7},{7,6},{8,9},{9,8},{10,11... | collective-permute-start | bytes 4915208 | tf_op jit(solution)/shard_map/ppermute | solution.py:327
  22.2 18.2 %all-to-all-start = ((bf16[8,4,32,128]{3,2,1,0:T(8,128)(2,1)}), bf16[8,4,32,128]{3,2,1,0:T(8,128)(2,1)S(1)}, u32[]{:S(2)}, u32[]{:S(2)}) async-start(bf16[8,4,32,128]{3,2,1,0:T(8,128)(2,1)} %add_convert_fusion), calls=%async_computation | async-start | bytes 524288 | tf_op jit(solution)/shard_map/all_to_all | solution.py:330
  26.6 12.9 %collective-permute-start.1 = (bf16[2,32,3200]{2,1,0:T(8,128)(2,1)S(1)}, bf16[2,32,3200]{2,1,0:T(8,128)(2,1)S(1)}, u32[]{:S(2)}, u32[]{:S(2)}) collective-permute-start(bf16[2,32,3200]{2,1,0:T(8,128)(2,1)S(1)} %collective-permute-done.refs_3_.refs_2_), channel_id=1, source_target_pairs={{0,2},{1,15},{2,4},{3,1},{4,6},{5,3},{6,8},{7,5},{8,10},{9,7},{10,... | collective-permute-start | bytes 1228808 | tf_op jit(solution)/shard_map/ppermute | solution.py:339
  29.3 14.6 %collective-permute-start.7 = (bf16[2,32,3200]{2,1,0:T(8,128)(2,1)S(1)}, bf16[2,32,3200]{2,1,0:T(8,128)(2,1)S(1)}, u32[]{:S(2)}, u32[]{:S(2)}) collective-permute-start(bf16[2,32,3200]{2,1,0:T(8,128)(2,1)S(1)} %collective-permute-done.6.refs_6_.refs_5_), channel_id=1, source_target_pairs={{0,2},{1,15},{2,4},{3,1},{4,6},{5,3},{6,8},{7,5},{8,10},{9,7},{10,... | collective-permute-start | bytes 1228808 | tf_op jit(solution)/shard_map/ppermute | solution.py:339
  39.5 8.9 %collective-permute-start.2 = (bf16[2,32,3200]{2,1,0:T(8,128)(2,1)S(1)}, bf16[2,32,3200]{2,1,0:T(8,128)(2,1)}, u32[]{:S(2)}, u32[]{:S(2)}) collective-permute-start(bf16[2,32,3200]{2,1,0:T(8,128)(2,1)S(1)} %collective-permute-done.1.refs_5_.refs_4_), channel_id=1, source_target_pairs={{0,2},{1,15},{2,4},{3,1},{4,6},{5,3},{6,8},{7,5},{8,10},{9,7},{10,... | collective-permute-start | bytes 1228808 | tf_op jit(solution)/shard_map/ppermute | solution.py:339
  43.9 8.9 %collective-permute-start.12 = (bf16[2,32,3200]{2,1,0:T(8,128)(2,1)S(1)}, bf16[2,32,3200]{2,1,0:T(8,128)(2,1)}, u32[]{:S(2)}, u32[]{:S(2)}) collective-permute-start(bf16[2,32,3200]{2,1,0:T(8,128)(2,1)S(1)} %collective-permute-done.7.refs_8_.refs_7_), channel_id=1, source_target_pairs={{0,2},{1,15},{2,4},{3,1},{4,6},{5,3},{6,8},{7,5},{8,10},{9,7},{10,... | collective-permute-start | bytes 1228808 | tf_op jit(solution)/shard_map/ppermute | solution.py:339
  48.4 10.4 %collective-permute-start.3 = (bf16[2,32,3200]{2,1,0:T(8,128)(2,1)}, bf16[2,32,3200]{2,1,0:T(8,128)(2,1)}, u32[]{:S(2)}, u32[]{:S(2)}) collective-permute-start(bf16[2,32,3200]{2,1,0:T(8,128)(2,1)} %collective-permute-done.2.refs_7_.refs_6_), channel_id=1, source_target_pairs={{0,2},{1,15},{2,4},{3,1},{4,6},{5,3},{6,8},{7,5},{8,10},{9,7},{10,... | collective-permute-start | bytes 1228808 | tf_op jit(solution)/shard_map/ppermute | solution.py:339
  52.8 8.8 %collective-permute-start.13 = (bf16[2,32,3200]{2,1,0:T(8,128)(2,1)}, bf16[2,32,3200]{2,1,0:T(8,128)(2,1)}, u32[]{:S(2)}, u32[]{:S(2)}) collective-permute-start(bf16[2,32,3200]{2,1,0:T(8,128)(2,1)} %collective-permute-done.12.refs_2_.refs_9_), channel_id=1, source_target_pairs={{0,2},{1,15},{2,4},{3,1},{4,6},{5,3},{6,8},{7,5},{8,10},{9,7},{10,... | collective-permute-start | bytes 1228808 | tf_op jit(solution)/shard_map/ppermute | solution.py:339
  53.7 43.0 %all-to-all-start.1 = ((bf16[8,4,64,384]{3,2,1,0:T(8,128)(2,1)}), bf16[8,4,64,384]{3,2,1,0:T(8,128)(2,1)S(1)}, u32[]{:S(2)}, u32[]{:S(2)}) async-start(bf16[8,4,64,384]{3,2,1,0:T(8,128)(2,1)} %shard_map.97), calls=%async_computation.1 | async-start | bytes 3145728 | tf_op jit(solution)/shard_map/all_to_all | solution.py:333
  58.8 14.4 %collective-permute-start.4 = (bf16[2,32,3200]{2,1,0:T(8,128)(2,1)}, bf16[2,32,3200]{2,1,0:T(8,128)(2,1)S(1)}, u32[]{:S(2)}, u32[]{:S(2)}) collective-permute-start(bf16[2,32,3200]{2,1,0:T(8,128)(2,1)} %collective-permute-done.3.refs_1_.refs_8_), channel_id=1, source_target_pairs={{0,2},{1,15},{2,4},{3,1},{4,6},{5,3},{6,8},{7,5},{8,10},{9,7},{10,... | collective-permute-start | bytes 1228808 | tf_op jit(solution)/shard_map/ppermute | solution.py:339
  61.6 18.4 %collective-permute-start.14 = (bf16[2,32,3200]{2,1,0:T(8,128)(2,1)}, bf16[2,32,3200]{2,1,0:T(8,128)(2,1)S(1)}, u32[]{:S(2)}, u32[]{:S(2)}) collective-permute-start(bf16[2,32,3200]{2,1,0:T(8,128)(2,1)} %collective-permute-done.13.refs_4_.refs_11_), channel_id=1, source_target_pairs={{0,2},{1,15},{2,4},{3,1},{4,6},{5,3},{6,8},{7,5},{8,10},{9,7},{10,... | collective-permute-start | bytes 1228808 | tf_op jit(solution)/shard_map/ppermute | solution.py:339
  73.2 8.1 %collective-permute-start.11 = (bf16[2,32,3200]{2,1,0:T(8,128)(2,1)S(1)}, bf16[2,32,3200]{2,1,0:T(8,128)(2,1)S(1)}, u32[]{:S(2)}, u32[]{:S(2)}) collective-permute-start(bf16[2,32,3200]{2,1,0:T(8,128)(2,1)S(1)} %collective-permute-done.4.refs_3_.refs_10_), channel_id=1, source_target_pairs={{0,2},{1,15},{2,4},{3,1},{4,6},{5,3},{6,8},{7,5},{8,10},{9,7},{10,... | collective-permute-start | bytes 1228808 | tf_op jit(solution)/shard_map/ppermute | solution.py:339
  80.0 7.2 %collective-permute-start.16 = (bf16[2,32,3200]{2,1,0:T(8,128)(2,1)S(1)}, bf16[2,32,3200]{2,1,0:T(8,128)(2,1)S(1)}, u32[]{:S(2)}, u32[]{:S(2)}) collective-permute-start(bf16[2,32,3200]{2,1,0:T(8,128)(2,1)S(1)} %collective-permute-done.14.refs_2_.refs_13_), channel_id=1, source_target_pairs={{0,2},{1,15},{2,4},{3,1},{4,6},{5,3},{6,8},{7,5},{8,10},{9,7},{10,... | collective-permute-start | bytes 1228808 | tf_op jit(solution)/shard_map/ppermute | solution.py:339
  81.3 10.3 %collective-permute-start.15 = (bf16[2,32,3200]{2,1,0:T(8,128)(2,1)S(1)}, bf16[2,32,3200]{2,1,0:T(8,128)(2,1)S(1)}, u32[]{:S(2)}, u32[]{:S(2)}) collective-permute-start(bf16[2,32,3200]{2,1,0:T(8,128)(2,1)S(1)} %collective-permute-done.11.refs_1_.refs_12_), channel_id=1, source_target_pairs={{0,2},{1,15},{2,4},{3,1},{4,6},{5,3},{6,8},{7,5},{8,10},{9,7},{10,... | collective-permute-start | bytes 1228808 | tf_op jit(solution)/shard_map/ppermute | solution.py:339
  96.7 14.3 %all-to-all-start.2 = ((bf16[8,4,32,128]{3,2,1,0:T(8,128)(2,1)}), bf16[8,4,32,128]{3,2,1,0:T(8,128)(2,1)S(1)}, u32[]{:S(2)}, u32[]{:S(2)}) async-start(bf16[8,4,32,128]{3,2,1,0:T(8,128)(2,1)} %get-tuple-element.51), calls=%async_computation.2 | async-start | bytes 524288 | tf_op jit(solution)/shard_map/all_to_all | solution.py:333
  111.7 39.0 %collective-permute-start.26 = (f32[4,64,3200]{2,1,0:T(8,128)}, f32[4,64,3200]{2,1,0:T(8,128)}, u32[]{:S(2)}, u32[]{:S(2)}) collective-permute-start(f32[4,64,3200]{2,1,0:T(8,128)} %get-tuple-element.61), channel_id=1, source_target_pairs={{0,1},{1,0},{2,3},{3,2},{4,5},{5,4},{6,7},{7,6},{8,9},{9,8},{10,11... | collective-permute-start | bytes 9830408 | tf_op jit(solution)/shard_map/ppermute | solution.py:327
  115.6 24.1 %all-to-all-start.3 = ((bf16[8,4,32,640]{3,2,1,0:T(8,128)(2,1)}), bf16[8,4,32,640]{3,2,1,0:T(8,128)(2,1)S(1)}, u32[]{:S(2)}, u32[]{:S(2)}) async-start(bf16[8,4,32,640]{3,2,1,0:T(8,128)(2,1)} %get-tuple-element.56), calls=%async_computation.3 | async-start | bytes 2621440 | tf_op jit(solution)/shard_map/all_to_all | solution.py:333
  121.0 4.4 %collective-permute-start.23 = (bf16[4,32,128]{2,1,0:T(8,128)(2,1)S(1)}, bf16[4,32,128]{2,1,0:T(8,128)(2,1)S(1)}, u32[]{:S(2)}, u32[]{:S(2)}) collective-permute-start(bf16[4,32,128]{2,1,0:T(8,128)(2,1)S(1)} %shard_map.101.refs_0_), channel_id=1, source_target_pairs={{0,14},{1,15},{2,0},{3,1},{4,2},{5,3},{6,4},{7,5},{8,6},{9,7},{10,... | collective-permute-start | bytes 98312 | tf_op jit(solution)/shard_map/ppermute | solution.py:395
  121.6 6.8 %collective-permute-start.17 = (bf16[4,32,128]{2,1,0:T(8,128)(2,1)S(1)}, bf16[4,32,128]{2,1,0:T(8,128)(2,1)S(1)}, u32[]{:S(2)}, u32[]{:S(2)}) collective-permute-start(bf16[4,32,128]{2,1,0:T(8,128)(2,1)S(1)} %shard_map.101.refs_0_), channel_id=1, source_target_pairs={{0,2},{1,3},{2,4},{3,5},{4,6},{5,7},{6,8},{7,9},{8,10},{9,11},{10,... | collective-permute-start | bytes 98312 | tf_op jit(solution)/shard_map/ppermute | solution.py:395
  122.5 8.5 %collective-permute-start.18 = (bf16[4,32,128]{2,1,0:T(8,128)(2,1)S(1)}, bf16[4,32,128]{2,1,0:T(8,128)(2,1)S(1)}, u32[]{:S(2)}, u32[]{:S(2)}) collective-permute-start(bf16[4,32,128]{2,1,0:T(8,128)(2,1)S(1)} %shard_map.101.refs_0_), channel_id=1, source_target_pairs={{0,4},{1,5},{2,6},{3,7},{4,8},{5,9},{6,10},{7,11},{8,12},{9,13},{1... | collective-permute-start | bytes 98312 | tf_op jit(solution)/shard_map/ppermute | solution.py:395
  124.1 15.6 %collective-permute-start.19 = (bf16[4,32,128]{2,1,0:T(8,128)(2,1)S(1)}, bf16[4,32,128]{2,1,0:T(8,128)(2,1)S(1)}, u32[]{:S(2)}, u32[]{:S(2)}) collective-permute-start(bf16[4,32,128]{2,1,0:T(8,128)(2,1)S(1)} %shard_map.101.refs_0_), channel_id=1, source_target_pairs={{0,6},{1,7},{2,8},{3,9},{4,10},{5,11},{6,12},{7,13},{8,14},{9,15},... | collective-permute-start | bytes 98312 | tf_op jit(solution)/shard_map/ppermute | solution.py:395
  125.4 14.4 %collective-permute-start.20 = (bf16[4,32,128]{2,1,0:T(8,128)(2,1)S(1)}, bf16[4,32,128]{2,1,0:T(8,128)(2,1)S(1)}, u32[]{:S(2)}, u32[]{:S(2)}) collective-permute-start(bf16[4,32,128]{2,1,0:T(8,128)(2,1)S(1)} %shard_map.101.refs_0_), channel_id=1, source_target_pairs={{0,8},{1,9},{2,10},{3,11},{4,12},{5,13},{6,14},{7,15},{8,0},{9,1},... | collective-permute-start | bytes 98312 | tf_op jit(solution)/shard_map/ppermute | solution.py:395
  128.4 11.3 %collective-permute-start.21 = (bf16[4,32,128]{2,1,0:T(8,128)(2,1)S(1)}, bf16[4,32,128]{2,1,0:T(8,128)(2,1)S(1)}, u32[]{:S(2)}, u32[]{:S(2)}) collective-permute-start(bf16[4,32,128]{2,1,0:T(8,128)(2,1)S(1)} %shard_map.101.refs_0_), channel_id=1, source_target_pairs={{0,10},{1,11},{2,12},{3,13},{4,14},{5,15},{6,0},{7,1},{8,2},{9,3},... | collective-permute-start | bytes 98312 | tf_op jit(solution)/shard_map/ppermute | solution.py:395
  131.0 8.8 %collective-permute-start.22 = (bf16[4,32,128]{2,1,0:T(8,128)(2,1)S(1)}, bf16[4,32,128]{2,1,0:T(8,128)(2,1)S(1)}, u32[]{:S(2)}, u32[]{:S(2)}) collective-permute-start(bf16[4,32,128]{2,1,0:T(8,128)(2,1)S(1)} %shard_map.101.refs_0_), channel_id=1, source_target_pairs={{0,12},{1,13},{2,14},{3,15},{4,0},{5,1},{6,2},{7,3},{8,4},{9,5},{1... | collective-permute-start | bytes 98312 | tf_op jit(solution)/shard_map/ppermute | solution.py:395
  141.1 5.2 %collective-permute-start.24 = (bf16[8,4,32,128]{3,2,1,0:T(8,128)(2,1)}, bf16[8,4,32,128]{3,2,1,0:T(8,128)(2,1)S(1)}, u32[]{:S(2)}, u32[]{:S(2)}) collective-permute-start(bf16[8,4,32,128]{3,2,1,0:T(8,128)(2,1)} %shard_map.102.mine), channel_id=1, source_target_pairs={{0,1},{1,0},{2,3},{3,2},{4,5},{5,4},{6,7},{7,6},{8,9},{9,8},{10,11... | collective-permute-start | bytes 786440 | tf_op jit(solution)/shard_map/ppermute | solution.py:327
  142.7 3.5 %collective-permute-start.25 = (f32[4,32,320]{2,1,0:T(8,128)S(1)}, f32[4,32,320]{2,1,0:T(8,128)S(1)}, u32[]{:S(2)}, u32[]{:S(2)}) collective-permute-start(f32[4,32,320]{2,1,0:T(8,128)S(1)} %get-tuple-element.59), channel_id=1, source_target_pairs={{0,1},{1,0},{2,3},{3,2},{4,5},{5,4},{6,7},{7,6},{8,9},{9,8},{10,11... | collective-permute-start | bytes 491528 | tf_op jit(solution)/shard_map/ppermute | solution.py:327
  142.8 12.2 %all-to-all-start.4 = ((bf16[8,4,32,128]{3,2,1,0:T(8,128)(2,1)}), bf16[8,4,32,128]{3,2,1,0:T(8,128)(2,1)S(1)}, u32[]{:S(2)}, u32[]{:S(2)}) async-start(bf16[8,4,32,128]{3,2,1,0:T(8,128)(2,1)} %shard_map.102.mine), calls=%async_computation.4 | async-start | bytes 524288 | tf_op jit(solution)/shard_map/all_to_all | solution.py:333
  (27 other events, 452.3 us)

commit v3 on v2

--- a/solution.py
+++ b/solution.py
@@ -378,10 +378,10 @@
     products = step_products((0, 1, 2, 3), place, sum(own[:4], []), weights, ())
     own[5][0] = after(own[5][0], *products)
     own.append(passed_on(own[5]))
-    products = step_products((4, 5), place, own[4] + own[5], weights, products)
-    own[6][1] = after(own[6][1], *products)
     own.append(passed_on(own[6]))
-    products = step_products((6, 7), place, own[6] + own[7], weights, products)
+    units = own[4] + own[5] + own[6]
+    products = step_products((4, 5, 6), place, units, weights, products)
+    products = step_products((7,), place, own[7], weights, products)
     main_parts, side_parts = products
 
     side_terms = over_rows(after(side_parts, shared))

time: 159 us -> 158 us (level)
  waiting for transfers between devices: 39.8 us -> 35.2 us
  starting transfers between devices: 67.1 us -> 69 us
    ppermute x14, waiting for transfers between devices: 32 us -> 28.1 us  [passed_on(): return [lax.ppermute(unit, 'col', RING) for unit in units]]
    unnamed x52 -> x56, local copies, waits for them, and re-layouts: 4.38 us -> 4.36 us
  transfers between devices with their start and end apart: 33 -> 33, of which waited for: 11 -> 10; matrix products, arithmetic and copies ran while one was open for 4% -> 4% of each run, Pallas kernels for 23% -> 24%
where the time goes in v3:
time: 158 us; the launch traced here: 157 us
  starting transfers between devices  69 us (44%)
  Pallas kernels  40.4 us (26%)
  waiting for transfers between devices  35.2 us (22%)
  local copies, waits for them, and re-layouts  5.67 us (4%)
  other arithmetic  5.58 us (4%)
    ppermute x14, waiting for transfers between devices, passed_on(): return [lax.ppermute(unit, 'col', RING) for unit in units]  28.1 us
    ppermute x14, starting transfers between devices, passed_on(): return [lax.ppermute(unit, 'col', RING) for unit in units]  24.9 us
    all_to_all x4, starting transfers between devices, over_rows(): return lax.all_to_all(pieces, 'row', 0, 0)  18.9 us
    pallas_call x3, Pallas kernels, step_products(): pl.pallas_call(kernel, out_shape=(jax.ShapeDtypeStruct((ROWS,) + main_sha...  17.4 us
    ppermute x7, starting transfers between devices, body(): lax.ppermute(factor, 'col', [(c, (c + 2 * hop) % 16) for c in range(16)])  12.8 us
    pallas_call x7, Pallas kernels, small_call(): pl.pallas_call(kernel, out_shape=out_shape, in_specs=[SMEM] * scalars + [...  10.5 us
    pallas_call x1, Pallas kernels, grad_b_parts(): pl.pallas_call(grad_b_kernel, out_shape=(part, part), in_specs=[SMEM, SME...  9.25 us
    ppermute x7, starting transfers between devices, swap(): return lax.ppermute(piece, 'col', SWAP)  7.93 us
  transfers between devices with their start and end apart: 33, of which 10 were waited for; matrix products, arithmetic and copies ran while one was open for 4% of the time, Pallas kernels for 24%

profile of v3, /device:TPU:1, one launch (start us, length us, event | category | flops | bytes accessed | tf_op | source)
XLA Modules:
  0.0 156.8 jit_solution(7977512104710693352)
XLA Ops:
  1.9 6.5 %collective-permute-start.5 = (bf16[2,32,3200]{2,1,0:T(8,128)(2,1)S(1)}, bf16[2,32,3200]{2,1,0:T(8,128)(2,1)S(1)}, u32[]{:S(2)}, u32[]{:S(2)}) collective-permute-start(bf16[2,32,3200]{2,1,0:T(8,128)(2,1)S(1)} %get-tuple-element.61.refs_2_.refs_1_), channel_id=1, source_target_pairs={{0,2},{1,15},{2,4},{3,1},{4,6},{5,3},{6,8},{7,5},{8,10},{9,7},{10,... | collective-permute-start | bytes 1228808 | tf_op jit(solution)/shard_map/ppermute | solution.py:339
  9.2 1.7 %copy-done.11 = bf16[4,320,1024]{2,1,0:T(8,128)(2,1)S(1)} copy-done((bf16[4,320,1024]{2,1,0:T(8,128)(2,1)S(1)}, bf16[4,320,1024]{2,1,0:T(8,128)(2,1)}, u32[]{:S(2)}) %copy-start.11) | copy-done | bytes 2621464
  13.3 4.4 %collective-permute-done.refs_3_.refs_2_ = bf16[2,32,3200]{2,1,0:T(8,128)(2,1)S(1)} collective-permute-done((bf16[2,32,3200]{2,1,0:T(8,128)(2,1)S(1)}, bf16[2,32,3200]{2,1,0:T(8,128)(2,1)S(1)}, u32[]{:S(2)}, u32[]{:S(2)}) %collective-permute-start) | collective-permute-done | bytes 409632 | tf_op jit(solution)/shard_map/ppermute | solution.py:339
  17.7 2.0 %collective-permute-start.9 = (bf16[320,3200]{1,0:T(8,128)(2,1)}, bf16[320,3200]{1,0:T(8,128)(2,1)}, u32[]{:S(2)}, u32[]{:S(2)}) collective-permute-start(bf16[320,3200]{1,0:T(8,128)(2,1)} %refs_0_), channel_id=1, source_target_pairs={{0,1},{1,0},{2,3},{3,2},{4,5},{5,4},{6,7},{7,6},{8,9},{9,8},{10,11... | collective-permute-start | bytes 6144008 | tf_op jit(solution)/shard_map/ppermute | solution.py:327
  22.2 4.4 %all-to-all-start = ((bf16[8,4,32,128]{3,2,1,0:T(8,128)(2,1)}), bf16[8,4,32,128]{3,2,1,0:T(8,128)(2,1)S(1)}, u32[]{:S(2)}, u32[]{:S(2)}) async-start(bf16[8,4,32,128]{3,2,1,0:T(8,128)(2,1)} %add_convert_fusion), calls=%async_computation | async-start | bytes 524288 | tf_op jit(solution)/shard_map/all_to_all | solution.py:330
  26.6 2.7 %collective-permute-start.1 = (bf16[2,32,3200]{2,1,0:T(8,128)(2,1)S(1)}, bf16[2,32,3200]{2,1,0:T(8,128)(2,1)S(1)}, u32[]{:S(2)}, u32[]{:S(2)}) collective-permute-start(bf16[2,32,3200]{2,1,0:T(8,128)(2,1)S(1)} %collective-permute-done.refs_3_.refs_2_), channel_id=1, source_target_pairs={{0,2},{1,15},{2,4},{3,1},{4,6},{5,3},{6,8},{7,5},{8,10},{9,7},{10,... | collective-permute-start | bytes 1228808 | tf_op jit(solution)/shard_map/ppermute | solution.py:339
  30.5 9.1 %collective-permute-done.1.refs_5_.refs_4_ = bf16[2,32,3200]{2,1,0:T(8,128)(2,1)S(1)} collective-permute-done((bf16[2,32,3200]{2,1,0:T(8,128)(2,1)S(1)}, bf16[2,32,3200]{2,1,0:T(8,128)(2,1)S(1)}, u32[]{:S(2)}, u32[]{:S(2)}) %collective-permute-start.1) | collective-permute-done | bytes 409632 | tf_op jit(solution)/shard_map/ppermute | solution.py:339
  40.4 3.6 %collective-permute-done.7.refs_8_.refs_7_ = bf16[2,32,3200]{2,1,0:T(8,128)(2,1)} collective-permute-done((bf16[2,32,3200]{2,1,0:T(8,128)(2,1)S(1)}, bf16[2,32,3200]{2,1,0:T(8,128)(2,1)}, u32[]{:S(2)}, u32[]{:S(2)}) %collective-permute-start.7) | collective-permute-done | bytes 409632 | tf_op jit(solution)/shard_map/ppermute | solution.py:339
  44.9 1.9 %shard_map.97 = bf16[8,4,64,384]{3,2,1,0:T(8,128)(2,1)} custom-call(s32[11]{0:T(128)S(1)} %concatenate.3.place.refs_0_, bf16[8,4,32,128]{3,2,1,0:T(8,128)(2,1)S(1)} %all-to-all-done.terms, bf16[4,64,320]{2,1,0:T(8,128)(2,1)S(1)} %copy-done.23), custom_call_target="tpu_custom_call" | custom-call | flops 3000000000 | bytes 8388608 | tf_op jit(solution)/shard_map/pallas_call | solution.py:145
  49.3 3.4 %collective-permute-done.13.refs_2_.refs_9_ = bf16[2,32,3200]{2,1,0:T(8,128)(2,1)S(1)} collective-permute-done((bf16[2,32,3200]{2,1,0:T(8,128)(2,1)}, bf16[2,32,3200]{2,1,0:T(8,128)(2,1)S(1)}, u32[]{:S(2)}, u32[]{:S(2)}) %collective-permute-start.13) | collective-permute-done | bytes 409632 | tf_op jit(solution)/shard_map/ppermute | solution.py:339
  53.6 5.0 %all-to-all-start.1 = ((bf16[8,4,64,384]{3,2,1,0:T(8,128)(2,1)}), bf16[8,4,64,384]{3,2,1,0:T(8,128)(2,1)S(1)}, u32[]{:S(2)}, u32[]{:S(2)}) async-start(bf16[8,4,64,384]{3,2,1,0:T(8,128)(2,1)} %shard_map.97), calls=%async_computation.1 | async-start | bytes 3145728 | tf_op jit(solution)/shard_map/all_to_all | solution.py:333
  58.7 1.8 %collective-permute-start.4 = (bf16[2,32,3200]{2,1,0:T(8,128)(2,1)S(1)}, bf16[2,32,3200]{2,1,0:T(8,128)(2,1)S(1)}, u32[]{:S(2)}, u32[]{:S(2)}) collective-permute-start(bf16[2,32,3200]{2,1,0:T(8,128)(2,1)S(1)} %collective-permute-done.3.refs_1_.refs_8_), channel_id=1, source_target_pairs={{0,2},{1,15},{2,4},{3,1},{4,6},{5,3},{6,8},{7,5},{8,10},{9,7},{10,... | collective-permute-start | bytes 1228808 | tf_op jit(solution)/shard_map/ppermute | solution.py:339
  62.5 3.2 %shard_map.95 = (bf16[320,3200]{1,0:T(8,128)(2,1)S(1)}, bf16[320,3200]{1,0:T(8,128)(2,1)S(1)}, bf16[256,3200]{1,0:T(8,128)(2,1)S(1)}, bf16[256,3200]{1,0:T(8,128)(2,1)S(1)}) custom-call(bf16[320,3200]{1,0:T(8,128)(2,1)} %refs_0_, bf16[320,3200]{1,0:T(8,128)(2,1)} %collective-permute-done.9.refs_1_, bf16[256,3200]{1,0:T(8,128)(2,1)} %bitcast.3.refs_2_, ...), custom_call_target="tpu_custom_call" | custom-call | flops 3000000000 | bytes 8388608 | tf_op jit(solution)/shard_map/pallas_call | solution.py:53
  65.7 7.6 %shard_map.96 = (bf16[8,4,32,640]{3,2,1,0:T(8,128)(2,1)}, bf16[8,4,32,128]{3,2,1,0:T(8,128)(2,1)}) custom-call(s32[11]{0:T(128)S(1)} %concatenate.3.place.refs_0_, bf16[2,32,3200]{2,1,0:T(8,128)(2,1)S(1)} %get-tuple-element.62.refs_1_.refs_0_, bf16[2,32,3200]{2,1,0:T(8,128)(2,1)S(1)} %get-tuple-element.61.refs_2_.refs_1_, ...), custom_call_target="tpu_custom_call" | custom-call | flops 3000000000 | bytes 8388608 | tf_op jit(solution)/shard_map/pallas_call | solution.py:122
  73.3 1.8 %collective-permute-start.11 = (bf16[2,32,3200]{2,1,0:T(8,128)(2,1)S(1)}, bf16[2,32,3200]{2,1,0:T(8,128)(2,1)S(1)}, u32[]{:S(2)}, u32[]{:S(2)}) collective-permute-start(bf16[2,32,3200]{2,1,0:T(8,128)(2,1)S(1)} %collective-permute-done.4.refs_3_.refs_10_), channel_id=1, source_target_pairs={{0,2},{1,15},{2,4},{3,1},{4,6},{5,3},{6,8},{7,5},{8,10},{9,7},{10,... | collective-permute-start | bytes 1228808 | tf_op jit(solution)/shard_map/ppermute | solution.py:339
  76.3 4.2 %collective-permute-done.11.refs_5_.refs_12_ = bf16[2,32,3200]{2,1,0:T(8,128)(2,1)S(1)} collective-permute-done((bf16[2,32,3200]{2,1,0:T(8,128)(2,1)S(1)}, bf16[2,32,3200]{2,1,0:T(8,128)(2,1)S(1)}, u32[]{:S(2)}, u32[]{:S(2)}) %collective-permute-start.11) | collective-permute-done | bytes 409632 | tf_op jit(solution)/shard_map/ppermute | solution.py:339
  80.5 2.7 %collective-permute-start.12 = (bf16[2,32,3200]{2,1,0:T(8,128)(2,1)S(1)}, bf16[2,32,3200]{2,1,0:T(8,128)(2,1)S(1)}, u32[]{:S(2)}, u32[]{:S(2)}) collective-permute-start(bf16[2,32,3200]{2,1,0:T(8,128)(2,1)S(1)} %collective-permute-done.11.refs_5_.refs_12_), channel_id=1, source_target_pairs={{0,2},{1,15},{2,4},{3,1},{4,6},{5,3},{6,8},{7,5},{8,10},{9,7},{10,... | collective-permute-start | bytes 1228808 | tf_op jit(solution)/shard_map/ppermute | solution.py:339
  83.7 6.1 %shard_map.98 = (bf16[8,4,32,640]{3,2,1,0:T(8,128)(2,1)}, bf16[8,4,32,128]{3,2,1,0:T(8,128)(2,1)}) custom-call(s32[11]{0:T(128)S(1)} %concatenate.3.place.refs_0_, bf16[2,32,3200]{2,1,0:T(8,128)(2,1)S(1)} %collective-permute-done.3.refs_1_.refs_8_, ...), custom_call_target="tpu_custom_call", output_to_operand_aliasing={{0}: (11, {}), {1}: (12, {})} | custom-call | flops 3000000000 | bytes 8388608 | tf_op jit(solution)/shard_map/pallas_call | solution.py:122
  89.9 3.8 %shard_map.99 = (bf16[8,4,32,640]{3,2,1,0:T(8,128)(2,1)}, bf16[8,4,32,128]{3,2,1,0:T(8,128)(2,1)}) custom-call(s32[11]{0:T(128)S(1)} %concatenate.3.place.refs_0_, bf16[2,32,3200]{2,1,0:T(8,128)(2,1)S(1)} %collective-permute-done.12.refs_1_.refs_14_, ...), custom_call_target="tpu_custom_call", output_to_operand_aliasing={{0}: (7, {}), {1}: (8, {})} | custom-call | flops 3000000000 | bytes 8388608 | tf_op jit(solution)/shard_map/pallas_call | solution.py:122
  94.4 5.0 %all-to-all-start.2 = ((bf16[8,4,32,128]{3,2,1,0:T(8,128)(2,1)}), bf16[8,4,32,128]{3,2,1,0:T(8,128)(2,1)S(1)}, u32[]{:S(2)}, u32[]{:S(2)}) async-start(bf16[8,4,32,128]{3,2,1,0:T(8,128)(2,1)} %get-tuple-element.49), calls=%async_computation.2 | async-start | bytes 524288 | tf_op jit(solution)/shard_map/all_to_all | solution.py:333
  99.5 9.3 %shard_map.100 = (f32[4,64,3200]{2,1,0:T(8,128)}, f32[4,64,3200]{2,1,0:T(8,128)}) custom-call(s32[11]{0:T(128)} %copy-done.9, f32[4]{0:T(128)} %convert_rsqrt_fusion.scales, bf16[8,4,64,384]{3,2,1,0:T(8,128)(2,1)} %copy-done, bf16[2,32,3200]{2,1,0:T(8,128)(2,1)} %copy-done.3, bf16[2,32,3200]{2,1,0:T(8,128)(2,1)} %copy-done.2, ...), custom_call_target="tpu_custom_call" | custom-call | flops 3000000000 | bytes 8388608 | tf_op jit(solution)/shard_map/pallas_call | solution.py:304
  109.4 4.3 %collective-permute-start.26 = (f32[4,64,3200]{2,1,0:T(8,128)}, f32[4,64,3200]{2,1,0:T(8,128)}, u32[]{:S(2)}, u32[]{:S(2)}) collective-permute-start(f32[4,64,3200]{2,1,0:T(8,128)} %get-tuple-element.59), channel_id=1, source_target_pairs={{0,1},{1,0},{2,3},{3,2},{4,5},{5,4},{6,7},{7,6},{8,9},{9,8},{10,11... | collective-permute-start | bytes 9830408 | tf_op jit(solution)/shard_map/ppermute | solution.py:327
  113.7 5.4 %all-to-all-start.3 = ((bf16[8,4,32,640]{3,2,1,0:T(8,128)(2,1)}), bf16[8,4,32,640]{3,2,1,0:T(8,128)(2,1)S(1)}, u32[]{:S(2)}, u32[]{:S(2)}) async-start(bf16[8,4,32,640]{3,2,1,0:T(8,128)(2,1)} %get-tuple-element.54), calls=%async_computation.3 | async-start | bytes 2621440 | tf_op jit(solution)/shard_map/all_to_all | solution.py:333
  121.4 2.5 %collective-permute-start.19 = (bf16[4,32,128]{2,1,0:T(8,128)(2,1)S(1)}, bf16[4,32,128]{2,1,0:T(8,128)(2,1)S(1)}, u32[]{:S(2)}, u32[]{:S(2)}) collective-permute-start(bf16[4,32,128]{2,1,0:T(8,128)(2,1)S(1)} %shard_map.101.refs_0_), channel_id=1, source_target_pairs={{0,6},{1,7},{2,8},{3,9},{4,10},{5,11},{6,12},{7,13},{8,14},{9,15},... | collective-permute-start | bytes 98312 | tf_op jit(solution)/shard_map/ppermute | solution.py:395
  123.9 2.2 %collective-permute-start.20 = (bf16[4,32,128]{2,1,0:T(8,128)(2,1)S(1)}, bf16[4,32,128]{2,1,0:T(8,128)(2,1)S(1)}, u32[]{:S(2)}, u32[]{:S(2)}) collective-permute-start(bf16[4,32,128]{2,1,0:T(8,128)(2,1)S(1)} %shard_map.101.refs_0_), channel_id=1, source_target_pairs={{0,8},{1,9},{2,10},{3,11},{4,12},{5,13},{6,14},{7,15},{8,0},{9,1},... | collective-permute-start | bytes 98312 | tf_op jit(solution)/shard_map/ppermute | solution.py:395
  126.1 2.2 %collective-permute-start.21 = (bf16[4,32,128]{2,1,0:T(8,128)(2,1)S(1)}, bf16[4,32,128]{2,1,0:T(8,128)(2,1)S(1)}, u32[]{:S(2)}, u32[]{:S(2)}) collective-permute-start(bf16[4,32,128]{2,1,0:T(8,128)(2,1)S(1)} %shard_map.101.refs_0_), channel_id=1, source_target_pairs={{0,10},{1,11},{2,12},{3,13},{4,14},{5,15},{6,0},{7,1},{8,2},{9,3},... | collective-permute-start | bytes 98312 | tf_op jit(solution)/shard_map/ppermute | solution.py:395
  128.4 3.6 %collective-permute-start.22 = (bf16[4,32,128]{2,1,0:T(8,128)(2,1)S(1)}, bf16[4,32,128]{2,1,0:T(8,128)(2,1)S(1)}, u32[]{:S(2)}, u32[]{:S(2)}) collective-permute-start(bf16[4,32,128]{2,1,0:T(8,128)(2,1)S(1)} %shard_map.101.refs_0_), channel_id=1, source_target_pairs={{0,12},{1,13},{2,14},{3,15},{4,0},{5,1},{6,2},{7,3},{8,4},{9,5},{1... | collective-permute-start | bytes 98312 | tf_op jit(solution)/shard_map/ppermute | solution.py:395
  131.9 5.9 %all-to-all-done.3.terms = bf16[8,4,32,640]{3,2,1,0:T(8,128)(2,1)S(1)} async-done(((bf16[8,4,32,640]{3,2,1,0:T(8,128)(2,1)}), bf16[8,4,32,640]{3,2,1,0:T(8,128)(2,1)S(1)}, u32[]{:S(2)}, u32[]{:S(2)}) %all-to-all-start.3) | async-done | bytes 1310752 | tf_op jit(solution)/shard_map/all_to_all | solution.py:333
  140.9 3.4 %all-to-all-start.4 = ((bf16[8,4,32,128]{3,2,1,0:T(8,128)(2,1)}), bf16[8,4,32,128]{3,2,1,0:T(8,128)(2,1)S(1)}, u32[]{:S(2)}, u32[]{:S(2)}) async-start(bf16[8,4,32,128]{3,2,1,0:T(8,128)(2,1)} %shard_map.102.mine), calls=%async_computation.4 | async-start | bytes 524288 | tf_op jit(solution)/shard_map/all_to_all | solution.py:333
  146.1 2.7 %shard_map.104 = bf16[4,64,320]{2,1,0:T(8,128)(2,1)} custom-call(s32[11]{0:T(128)S(1)} %copy-done.10, bf16[8,4,32,128]{3,2,1,0:T(8,128)(2,1)} %shard_map.102.mine, bf16[8,4,32,128]{3,2,1,0:T(8,128)(2,1)S(1)} %collective-permute-done.24.others, f32[4,32,320]{2,1,0:T(8,128)S(1)} %get-tuple-element.56.keep, f32[4,32,320]{2,1,0:T(8,128)S(1)} %collective-permute-done.25.got, ...), custom_call_target="tpu_custom_call" | custom-call | flops 3000000000 | bytes 8388608 | tf_op jit(solution)/shard_map/pallas_call | solution.py:145
  148.8 4.3 %add.13 = f32[4,64,3200]{2,1,0:T(8,128)} add(f32[4,64,3200]{2,1,0:T(8,128)S(1)} %copy-done.25, f32[4,64,3200]{2,1,0:T(8,128)} %collective-permute-done.26) | non-fusion elementwise | flops 819200 | bytes 9830400 | tf_op jit(solution)/shard_map/add | solution.py:413
  154.8 2.0 %shard_map.105 = f32[4,320,128]{2,1,0:T(8,128)} custom-call(s32[11]{0:T(128)S(1)} %copy-done.10, f32[4]{0:T(128)S(1)} %copy-done.24, bf16[8,4,32,128]{3,2,1,0:T(8,128)(2,1)S(1)} %all-to-all-done.4.mine, bf16[8,4,32,128]{3,2,1,0:T(8,128)(2,1)S(1)} %collective-permute-done.27.others, bf16[8,4,64,384]{3,2,1,0:T(8,128)(2,1)S(1)} %copy-done.1), custom_call_target="tpu_custom_call" | custom-call | flops 3000000000 | bytes 8388608 | tf_op jit(solution)/shard_map/pallas_call | solution.py:145
  (108 shorter events, 27.3 us)
Async XLA Ops:
  1.9 11.4 %collective-permute-start.5 = (bf16[2,32,3200]{2,1,0:T(8,128)(2,1)S(1)}, bf16[2,32,3200]{2,1,0:T(8,128)(2,1)S(1)}, u32[]{:S(2)}, u32[]{:S(2)}) collective-permute-start(bf16[2,32,3200]{2,1,0:T(8,128)(2,1)S(1)} %get-tuple-element.61.refs_2_.refs_1_), channel_id=1, source_target_pairs={{0,2},{1,15},{2,4},{3,1},{4,6},{5,3},{6,8},{7,5},{8,10},{9,7},{10,... | collective-permute-start | bytes 1228808 | tf_op jit(solution)/shard_map/ppermute | solution.py:339
  8.4 9.3 %collective-permute-start = (bf16[2,32,3200]{2,1,0:T(8,128)(2,1)S(1)}, bf16[2,32,3200]{2,1,0:T(8,128)(2,1)S(1)}, u32[]{:S(2)}, u32[]{:S(2)}) collective-permute-start(bf16[2,32,3200]{2,1,0:T(8,128)(2,1)S(1)} %get-tuple-element.62.refs_1_.refs_0_), channel_id=1, source_target_pairs={{0,2},{1,15},{2,4},{3,1},{4,6},{5,3},{6,8},{7,5},{8,10},{9,7},{10,... | collective-permute-start | bytes 1228808 | tf_op jit(solution)/shard_map/ppermute | solution.py:339
  12.2 9.3 %collective-permute-start.8 = (f32[8,4,32,128]{3,2,1,0:T(8,128)S(1)}, f32[8,4,32,128]{3,2,1,0:T(8,128)S(1)}, u32[]{:S(2)}, u32[]{:S(2)}) collective-permute-start(f32[8,4,32,128]{3,2,1,0:T(8,128)S(1)} %get-tuple-element.34), channel_id=1, source_target_pairs={{0,1},{1,0},{2,3},{3,2},{4,5},{5,4},{6,7},{7,6},{8,9},{9,8},{10,11... | collective-permute-start | bytes 1572872 | tf_op jit(solution)/shard_map/ppermute | solution.py:327
  17.7 44.8 %collective-permute-start.9 = (bf16[320,3200]{1,0:T(8,128)(2,1)}, bf16[320,3200]{1,0:T(8,128)(2,1)}, u32[]{:S(2)}, u32[]{:S(2)}) collective-permute-start(bf16[320,3200]{1,0:T(8,128)(2,1)} %refs_0_), channel_id=1, source_target_pairs={{0,1},{1,0},{2,3},{3,2},{4,5},{5,4},{6,7},{7,6},{8,9},{9,8},{10,11... | collective-permute-start | bytes 6144008 | tf_op jit(solution)/shard_map/ppermute | solution.py:327
  19.7 9.6 %collective-permute-start.6 = (bf16[2,32,3200]{2,1,0:T(8,128)(2,1)S(1)}, bf16[2,32,3200]{2,1,0:T(8,128)(2,1)S(1)}, u32[]{:S(2)}, u32[]{:S(2)}) collective-permute-start(bf16[2,32,3200]{2,1,0:T(8,128)(2,1)S(1)} %collective-permute-done.5.refs_4_.refs_3_), channel_id=1, source_target_pairs={{0,2},{1,15},{2,4},{3,1},{4,6},{5,3},{6,8},{7,5},{8,10},{9,7},{10,... | collective-permute-start | bytes 1228808 | tf_op jit(solution)/shard_map/ppermute | solution.py:339
  21.4 41.1 %collective-permute-start.10 = (bf16[256,3200]{1,0:T(8,128)(2,1)}, bf16[256,3200]{1,0:T(8,128)(2,1)}, u32[]{:S(2)}, u32[]{:S(2)}) collective-permute-start(bf16[256,3200]{1,0:T(8,128)(2,1)} %bitcast.3.refs_2_), channel_id=1, source_target_pairs={{0,1},{1,0},{2,3},{3,2},{4,5},{5,4},{6,7},{7,6},{8,9},{9,8},{10,11... | collective-permute-start | bytes 4915208 | tf_op jit(solution)/shard_map/ppermute | solution.py:327
  22.2 18.2 %all-to-all-start = ((bf16[8,4,32,128]{3,2,1,0:T(8,128)(2,1)}), bf16[8,4,32,128]{3,2,1,0:T(8,128)(2,1)S(1)}, u32[]{:S(2)}, u32[]{:S(2)}) async-start(bf16[8,4,32,128]{3,2,1,0:T(8,128)(2,1)} %add_convert_fusion), calls=%async_computation | async-start | bytes 524288 | tf_op jit(solution)/shard_map/all_to_all | solution.py:330
  26.6 12.9 %collective-permute-start.1 = (bf16[2,32,3200]{2,1,0:T(8,128)(2,1)S(1)}, bf16[2,32,3200]{2,1,0:T(8,128)(2,1)S(1)}, u32[]{:S(2)}, u32[]{:S(2)}) collective-permute-start(bf16[2,32,3200]{2,1,0:T(8,128)(2,1)S(1)} %collective-permute-done.refs_3_.refs_2_), channel_id=1, source_target_pairs={{0,2},{1,15},{2,4},{3,1},{4,6},{5,3},{6,8},{7,5},{8,10},{9,7},{10,... | collective-permute-start | bytes 1228808 | tf_op jit(solution)/shard_map/ppermute | solution.py:339
  29.3 14.7 %collective-permute-start.7 = (bf16[2,32,3200]{2,1,0:T(8,128)(2,1)S(1)}, bf16[2,32,3200]{2,1,0:T(8,128)(2,1)}, u32[]{:S(2)}, u32[]{:S(2)}) collective-permute-start(bf16[2,32,3200]{2,1,0:T(8,128)(2,1)S(1)} %collective-permute-done.6.refs_6_.refs_5_), channel_id=1, source_target_pairs={{0,2},{1,15},{2,4},{3,1},{4,6},{5,3},{6,8},{7,5},{8,10},{9,7},{10,... | collective-permute-start | bytes 1228808 | tf_op jit(solution)/shard_map/ppermute | solution.py:339
  39.5 8.9 %collective-permute-start.2 = (bf16[2,32,3200]{2,1,0:T(8,128)(2,1)S(1)}, bf16[2,32,3200]{2,1,0:T(8,128)(2,1)}, u32[]{:S(2)}, u32[]{:S(2)}) collective-permute-start(bf16[2,32,3200]{2,1,0:T(8,128)(2,1)S(1)} %collective-permute-done.1.refs_5_.refs_4_), channel_id=1, source_target_pairs={{0,2},{1,15},{2,4},{3,1},{4,6},{5,3},{6,8},{7,5},{8,10},{9,7},{10,... | collective-permute-start | bytes 1228808 | tf_op jit(solution)/shard_map/ppermute | solution.py:339
  44.0 8.7 %collective-permute-start.13 = (bf16[2,32,3200]{2,1,0:T(8,128)(2,1)}, bf16[2,32,3200]{2,1,0:T(8,128)(2,1)S(1)}, u32[]{:S(2)}, u32[]{:S(2)}) collective-permute-start(bf16[2,32,3200]{2,1,0:T(8,128)(2,1)} %collective-permute-done.7.refs_8_.refs_7_), channel_id=1, source_target_pairs={{0,2},{1,15},{2,4},{3,1},{4,6},{5,3},{6,8},{7,5},{8,10},{9,7},{10,... | collective-permute-start | bytes 1228808 | tf_op jit(solution)/shard_map/ppermute | solution.py:339
  48.4 10.3 %collective-permute-start.3 = (bf16[2,32,3200]{2,1,0:T(8,128)(2,1)}, bf16[2,32,3200]{2,1,0:T(8,128)(2,1)S(1)}, u32[]{:S(2)}, u32[]{:S(2)}) collective-permute-start(bf16[2,32,3200]{2,1,0:T(8,128)(2,1)} %collective-permute-done.2.refs_7_.refs_6_), channel_id=1, source_target_pairs={{0,2},{1,15},{2,4},{3,1},{4,6},{5,3},{6,8},{7,5},{8,10},{9,7},{10,... | collective-permute-start | bytes 1228808 | tf_op jit(solution)/shard_map/ppermute | solution.py:339
  52.7 8.9 %collective-permute-start.14 = (bf16[2,32,3200]{2,1,0:T(8,128)(2,1)S(1)}, bf16[2,32,3200]{2,1,0:T(8,128)(2,1)}, u32[]{:S(2)}, u32[]{:S(2)}) collective-permute-start(bf16[2,32,3200]{2,1,0:T(8,128)(2,1)S(1)} %collective-permute-done.13.refs_2_.refs_9_), channel_id=1, source_target_pairs={{0,2},{1,15},{2,4},{3,1},{4,6},{5,3},{6,8},{7,5},{8,10},{9,7},{10,... | collective-permute-start | bytes 1228808 | tf_op jit(solution)/shard_map/ppermute | solution.py:339
  53.6 40.8 %all-to-all-start.1 = ((bf16[8,4,64,384]{3,2,1,0:T(8,128)(2,1)}), bf16[8,4,64,384]{3,2,1,0:T(8,128)(2,1)S(1)}, u32[]{:S(2)}, u32[]{:S(2)}) async-start(bf16[8,4,64,384]{3,2,1,0:T(8,128)(2,1)} %shard_map.97), calls=%async_computation.1 | async-start | bytes 3145728 | tf_op jit(solution)/shard_map/all_to_all | solution.py:333
  58.7 14.6 %collective-permute-start.4 = (bf16[2,32,3200]{2,1,0:T(8,128)(2,1)S(1)}, bf16[2,32,3200]{2,1,0:T(8,128)(2,1)S(1)}, u32[]{:S(2)}, u32[]{:S(2)}) collective-permute-start(bf16[2,32,3200]{2,1,0:T(8,128)(2,1)S(1)} %collective-permute-done.3.refs_1_.refs_8_), channel_id=1, source_target_pairs={{0,2},{1,15},{2,4},{3,1},{4,6},{5,3},{6,8},{7,5},{8,10},{9,7},{10,... | collective-permute-start | bytes 1228808 | tf_op jit(solution)/shard_map/ppermute | solution.py:339
  61.6 13.6 %collective-permute-start.15 = (bf16[2,32,3200]{2,1,0:T(8,128)(2,1)}, bf16[2,32,3200]{2,1,0:T(8,128)(2,1)S(1)}, u32[]{:S(2)}, u32[]{:S(2)}) collective-permute-start(bf16[2,32,3200]{2,1,0:T(8,128)(2,1)} %collective-permute-done.14.refs_4_.refs_11_), channel_id=1, source_target_pairs={{0,2},{1,15},{2,4},{3,1},{4,6},{5,3},{6,8},{7,5},{8,10},{9,7},{10,... | collective-permute-start | bytes 1228808 | tf_op jit(solution)/shard_map/ppermute | solution.py:339
  73.3 7.2 %collective-permute-start.11 = (bf16[2,32,3200]{2,1,0:T(8,128)(2,1)S(1)}, bf16[2,32,3200]{2,1,0:T(8,128)(2,1)S(1)}, u32[]{:S(2)}, u32[]{:S(2)}) collective-permute-start(bf16[2,32,3200]{2,1,0:T(8,128)(2,1)S(1)} %collective-permute-done.4.refs_3_.refs_10_), channel_id=1, source_target_pairs={{0,2},{1,15},{2,4},{3,1},{4,6},{5,3},{6,8},{7,5},{8,10},{9,7},{10,... | collective-permute-start | bytes 1228808 | tf_op jit(solution)/shard_map/ppermute | solution.py:339
  75.2 14.7 %collective-permute-start.16 = (bf16[2,32,3200]{2,1,0:T(8,128)(2,1)S(1)}, bf16[2,32,3200]{2,1,0:T(8,128)(2,1)S(1)}, u32[]{:S(2)}, u32[]{:S(2)}) collective-permute-start(bf16[2,32,3200]{2,1,0:T(8,128)(2,1)S(1)} %collective-permute-done.15.refs_6_.refs_13_), channel_id=1, source_target_pairs={{0,2},{1,15},{2,4},{3,1},{4,6},{5,3},{6,8},{7,5},{8,10},{9,7},{10,... | collective-permute-start | bytes 1228808 | tf_op jit(solution)/shard_map/ppermute | solution.py:339
  80.5 9.3 %collective-permute-start.12 = (bf16[2,32,3200]{2,1,0:T(8,128)(2,1)S(1)}, bf16[2,32,3200]{2,1,0:T(8,128)(2,1)S(1)}, u32[]{:S(2)}, u32[]{:S(2)}) collective-permute-start(bf16[2,32,3200]{2,1,0:T(8,128)(2,1)S(1)} %collective-permute-done.11.refs_5_.refs_12_), channel_id=1, source_target_pairs={{0,2},{1,15},{2,4},{3,1},{4,6},{5,3},{6,8},{7,5},{8,10},{9,7},{10,... | collective-permute-start | bytes 1228808 | tf_op jit(solution)/shard_map/ppermute | solution.py:339
  94.4 14.3 %all-to-all-start.2 = ((bf16[8,4,32,128]{3,2,1,0:T(8,128)(2,1)}), bf16[8,4,32,128]{3,2,1,0:T(8,128)(2,1)S(1)}, u32[]{:S(2)}, u32[]{:S(2)}) async-start(bf16[8,4,32,128]{3,2,1,0:T(8,128)(2,1)} %get-tuple-element.49), calls=%async_computation.2 | async-start | bytes 524288 | tf_op jit(solution)/shard_map/all_to_all | solution.py:333
  109.4 39.4 %collective-permute-start.26 = (f32[4,64,3200]{2,1,0:T(8,128)}, f32[4,64,3200]{2,1,0:T(8,128)}, u32[]{:S(2)}, u32[]{:S(2)}) collective-permute-start(f32[4,64,3200]{2,1,0:T(8,128)} %get-tuple-element.59), channel_id=1, source_target_pairs={{0,1},{1,0},{2,3},{3,2},{4,5},{5,4},{6,7},{7,6},{8,9},{9,8},{10,11... | collective-permute-start | bytes 9830408 | tf_op jit(solution)/shard_map/ppermute | solution.py:327
  113.7 24.1 %all-to-all-start.3 = ((bf16[8,4,32,640]{3,2,1,0:T(8,128)(2,1)}), bf16[8,4,32,640]{3,2,1,0:T(8,128)(2,1)S(1)}, u32[]{:S(2)}, u32[]{:S(2)}) async-start(bf16[8,4,32,640]{3,2,1,0:T(8,128)(2,1)} %get-tuple-element.54), calls=%async_computation.3 | async-start | bytes 2621440 | tf_op jit(solution)/shard_map/all_to_all | solution.py:333
  119.1 4.8 %collective-permute-start.23 = (bf16[4,32,128]{2,1,0:T(8,128)(2,1)S(1)}, bf16[4,32,128]{2,1,0:T(8,128)(2,1)S(1)}, u32[]{:S(2)}, u32[]{:S(2)}) collective-permute-start(bf16[4,32,128]{2,1,0:T(8,128)(2,1)S(1)} %shard_map.101.refs_0_), channel_id=1, source_target_pairs={{0,14},{1,15},{2,0},{3,1},{4,2},{5,3},{6,4},{7,5},{8,6},{9,7},{10,... | collective-permute-start | bytes 98312 | tf_op jit(solution)/shard_map/ppermute | solution.py:395
  120.5 5.7 %collective-permute-start.17 = (bf16[4,32,128]{2,1,0:T(8,128)(2,1)S(1)}, bf16[4,32,128]{2,1,0:T(8,128)(2,1)S(1)}, u32[]{:S(2)}, u32[]{:S(2)}) collective-permute-start(bf16[4,32,128]{2,1,0:T(8,128)(2,1)S(1)} %shard_map.101.refs_0_), channel_id=1, source_target_pairs={{0,2},{1,3},{2,4},{3,5},{4,6},{5,7},{6,8},{7,9},{8,10},{9,11},{10,... | collective-permute-start | bytes 98312 | tf_op jit(solution)/shard_map/ppermute | solution.py:395
  120.6 7.8 %collective-permute-start.18 = (bf16[4,32,128]{2,1,0:T(8,128)(2,1)S(1)}, bf16[4,32,128]{2,1,0:T(8,128)(2,1)S(1)}, u32[]{:S(2)}, u32[]{:S(2)}) collective-permute-start(bf16[4,32,128]{2,1,0:T(8,128)(2,1)S(1)} %shard_map.101.refs_0_), channel_id=1, source_target_pairs={{0,4},{1,5},{2,6},{3,7},{4,8},{5,9},{6,10},{7,11},{8,12},{9,13},{1... | collective-permute-start | bytes 98312 | tf_op jit(solution)/shard_map/ppermute | solution.py:395
  121.4 16.5 %collective-permute-start.19 = (bf16[4,32,128]{2,1,0:T(8,128)(2,1)S(1)}, bf16[4,32,128]{2,1,0:T(8,128)(2,1)S(1)}, u32[]{:S(2)}, u32[]{:S(2)}) collective-permute-start(bf16[4,32,128]{2,1,0:T(8,128)(2,1)S(1)} %shard_map.101.refs_0_), channel_id=1, source_target_pairs={{0,6},{1,7},{2,8},{3,9},{4,10},{5,11},{6,12},{7,13},{8,14},{9,15},... | collective-permute-start | bytes 98312 | tf_op jit(solution)/shard_map/ppermute | solution.py:395
  123.9 13.9 %collective-permute-start.20 = (bf16[4,32,128]{2,1,0:T(8,128)(2,1)S(1)}, bf16[4,32,128]{2,1,0:T(8,128)(2,1)S(1)}, u32[]{:S(2)}, u32[]{:S(2)}) collective-permute-start(bf16[4,32,128]{2,1,0:T(8,128)(2,1)S(1)} %shard_map.101.refs_0_), channel_id=1, source_target_pairs={{0,8},{1,9},{2,10},{3,11},{4,12},{5,13},{6,14},{7,15},{8,0},{9,1},... | collective-permute-start | bytes 98312 | tf_op jit(solution)/shard_map/ppermute | solution.py:395
  126.1 11.7 %collective-permute-start.21 = (bf16[4,32,128]{2,1,0:T(8,128)(2,1)S(1)}, bf16[4,32,128]{2,1,0:T(8,128)(2,1)S(1)}, u32[]{:S(2)}, u32[]{:S(2)}) collective-permute-start(bf16[4,32,128]{2,1,0:T(8,128)(2,1)S(1)} %shard_map.101.refs_0_), channel_id=1, source_target_pairs={{0,10},{1,11},{2,12},{3,13},{4,14},{5,15},{6,0},{7,1},{8,2},{9,3},... | collective-permute-start | bytes 98312 | tf_op jit(solution)/shard_map/ppermute | solution.py:395
  128.4 9.5 %collective-permute-start.22 = (bf16[4,32,128]{2,1,0:T(8,128)(2,1)S(1)}, bf16[4,32,128]{2,1,0:T(8,128)(2,1)S(1)}, u32[]{:S(2)}, u32[]{:S(2)}) collective-permute-start(bf16[4,32,128]{2,1,0:T(8,128)(2,1)S(1)} %shard_map.101.refs_0_), channel_id=1, source_target_pairs={{0,12},{1,13},{2,14},{3,15},{4,0},{5,1},{6,2},{7,3},{8,4},{9,5},{1... | collective-permute-start | bytes 98312 | tf_op jit(solution)/shard_map/ppermute | solution.py:395
  139.2 5.2 %collective-permute-start.24 = (bf16[8,4,32,128]{3,2,1,0:T(8,128)(2,1)}, bf16[8,4,32,128]{3,2,1,0:T(8,128)(2,1)S(1)}, u32[]{:S(2)}, u32[]{:S(2)}) collective-permute-start(bf16[8,4,32,128]{3,2,1,0:T(8,128)(2,1)} %shard_map.102.mine), channel_id=1, source_target_pairs={{0,1},{1,0},{2,3},{3,2},{4,5},{5,4},{6,7},{7,6},{8,9},{9,8},{10,11... | collective-permute-start | bytes 786440 | tf_op jit(solution)/shard_map/ppermute | solution.py:327
  140.8 3.5 %collective-permute-start.25 = (f32[4,32,320]{2,1,0:T(8,128)S(1)}, f32[4,32,320]{2,1,0:T(8,128)S(1)}, u32[]{:S(2)}, u32[]{:S(2)}) collective-permute-start(f32[4,32,320]{2,1,0:T(8,128)S(1)} %get-tuple-element.57), channel_id=1, source_target_pairs={{0,1},{1,0},{2,3},{3,2},{4,5},{5,4},{6,7},{7,6},{8,9},{9,8},{10,11... | collective-permute-start | bytes 491528 | tf_op jit(solution)/shard_map/ppermute | solution.py:327
  140.9 12.2 %all-to-all-start.4 = ((bf16[8,4,32,128]{3,2,1,0:T(8,128)(2,1)}), bf16[8,4,32,128]{3,2,1,0:T(8,128)(2,1)S(1)}, u32[]{:S(2)}, u32[]{:S(2)}) async-start(bf16[8,4,32,128]{3,2,1,0:T(8,128)(2,1)} %shard_map.102.mine), calls=%async_computation.4 | async-start | bytes 524288 | tf_op jit(solution)/shard_map/all_to_all | solution.py:333
  (29 other events, 483.5 us)
